TPU v7x, 512 devices: a whole 4x4x16 slice. The times are simulated.
512 devices in a mesh: row: 32 (over y, z_lo, core), col: 16 (over x, z_hi).
Axes of the slice: x: 4, y: 4, z: 16 (z_hi: 4, z_lo: 4; z = z_hi * 4 + z_lo), core: 2. Of those that a mesh axis runs over, the one named last changes fastest.
Arguments:
- pair_map: bfloat16 [256, 256, 128], P('row', 'col'), may hold values from -6 to 6
- out_proj: bfloat16 [128, 512], replicated, may hold values from -0.5 to 0.5
- out_gate: bfloat16 [128, 128], replicated, may hold values from -0.5 to 0.5
- out_final: bfloat16 [128, 128], replicated, may hold values from -0.5 to 0.5
- in_proj: bfloat16 [128, 512], replicated, may hold values from -0.5 to 0.5
- in_gate: bfloat16 [128, 128], replicated, may hold values from -0.5 to 0.5
- in_final: bfloat16 [128, 128], replicated, may hold values from -0.5 to 0.5
Outputs:
- updated_map: bfloat16 [256, 256, 128], P('row', 'col')
All inputs are finite; a program needn't handle non-finite values.
Results may differ from a plain program's by a relative error of at most 0.015.
Values may be sent and summed in bfloat16 or wider, within the bound.
A program may use at most 64 MiB of HBM per device.

v0:
```python
import jax
import jax.numpy as jnp
from jax import lax
from jax.sharding import PartitionSpec as P


def from_root(block, axis, source):
    block = jnp.where(lax.axis_index(axis) == source, block, jnp.zeros_like(block))
    return lax.psum(block, axis)


def normalize(values):
    average = jnp.mean(values, axis=-1, keepdims=True)
    centred = values - average
    spread = jnp.mean(centred * centred, axis=-1, keepdims=True)
    return centred * lax.rsqrt(spread + 1e-05)


def prepare(pair_map, w_proj, w_gate, hidden):
    normed = normalize(pair_map.astype(jnp.float32)).astype(jnp.bfloat16)
    projected = jnp.dot(normed, w_proj, preferred_element_type=jnp.float32)
    left_side = (
        jax.nn.sigmoid(projected[..., 0:hidden]) * projected[..., hidden : 2 * hidden]
    ).astype(jnp.bfloat16)
    right_side = (
        jax.nn.sigmoid(projected[..., 2 * hidden : 3 * hidden]) * projected[..., 3 * hidden :]
    ).astype(jnp.bfloat16)
    gate_vals = jax.nn.sigmoid(jnp.dot(normed, w_gate, preferred_element_type=jnp.float32))
    return (left_side, right_side, gate_vals)


def finish(pair_map, summed, gate_vals, w_final):
    mixed_norm = normalize(summed).astype(jnp.bfloat16)
    update = gate_vals * jnp.dot(mixed_norm, w_final, preferred_element_type=jnp.float32)
    return (pair_map.astype(jnp.float32) + update).astype(jnp.bfloat16)


def body(pair_map, out_proj, out_gate, out_final, in_proj, in_gate, in_final):
    hidden = out_final.shape[0]
    fold_ratio = lax.axis_size("row") // lax.axis_size("col")
    row_id = lax.axis_index("row")
    col_id = lax.axis_index("col")
    row_count = pair_map.shape[0]
    left_side, right_side, gate_vals = prepare(pair_map, out_proj, out_gate, hidden)
    left_rows, right_rows = (
        lax.all_gather(left_side, "col", axis=1, tiled=True),
        lax.all_gather(right_side, "col", axis=1, tiled=True),
    )
    received = [
        from_root(right_rows, "row", col_id * fold_ratio + offset) for offset in range(fold_ratio)
    ]
    right_cols = jnp.concatenate(received, axis=0)
    summed = lax.dot_general(
        left_rows, right_cols, (((1,), (1,)), ((2,), (2,))), preferred_element_type=jnp.float32
    )
    after_out = finish(pair_map, jnp.transpose(summed, (1, 2, 0)), gate_vals, out_final)
    left_side, right_side, gate_vals = prepare(after_out, in_proj, in_gate, hidden)
    left_all, right_cols = (
        lax.all_gather(left_side, "row", axis=0, tiled=True),
        lax.all_gather(right_side, "row", axis=0, tiled=True),
    )
    own_block = lax.dynamic_slice_in_dim(left_all, row_id % fold_ratio * row_count, row_count, 1)
    left_cols = from_root(own_block, "col", row_id // fold_ratio)
    summed = lax.dot_general(
        left_cols, right_cols, (((0,), (0,)), ((2,), (2,))), preferred_element_type=jnp.float32
    )
    return finish(after_out, jnp.transpose(summed, (1, 2, 0)), gate_vals, in_final)


def solution(mesh):
    return jax.shard_map(
        body,
        mesh=mesh,
        in_specs=(P("row", "col", None), P(), P(), P(), P(), P(), P()),
        out_specs=P("row", "col", None),
        check_vma=False,
    )
```

profile of v0, /device:TPU:1, one launch (start us, length us, event | category | flops | bytes accessed | tf_op | source)
XLA Modules:
  0.0 705.3 jit_solution(7098569597779184596)
XLA Ops:
  6.5 0.0 copy-start
  6.5 0.0 copy-start.1
  6.5 0.0 copy-start.3
  6.5 0.0 copy-start.2
  6.5 0.0 all-reduce.6.cloned.1.call-start
  6.6 0.9 convert_reduce_fusion
  7.6 0.9 fusion.17
  8.5 0.0 copy-done
  8.5 1.0 fusion.13
  9.5 57.3 %all_gather.13 = bf16[8,256,128]{2,1,0:T(8,128)(2,1)S(1)} all-gather(bf16[8,16,128]{2,1,0:T(8,128)(2,1)S(1)} %get-tuple-element.11), channel_id=1, replica_groups=mesh['row'=32,'col'=16] {'col'}, dimensions={1}, use_global_device_ids=true | all-gather | bytes 557056 | tf_op jit(solution)/shard_map/all_gather | solution.py:47
  66.8 0.0 copy-start.5
  66.8 1.1 broadcast_select_fusion.2
  68.0 0.0 all-reduce.6.cloned.1.call-update
  68.0 0.0 all-gather.3.cloned.1.call-start
  68.0 44.7 %all_gather.12 = bf16[8,256,128]{2,1,0:T(8,128)(2,1)S(1)} all-gather(bf16[8,16,128]{2,1,0:T(8,128)(2,1)S(1)} %get-tuple-element.12), channel_id=1, replica_groups=mesh['row'=32,'col'=16] {'col'}, dimensions={1}, use_global_device_ids=true | all-gather | bytes 557056 | tf_op jit(solution)/shard_map/all_gather | solution.py:46
  112.7 0.4 copy.20
  113.1 1.0 fusion.7
  114.1 247.1 %all-reduce.6.cloned.1.call-done = (bf16[8,256,128]{2,1,0:T(8,128)(2,1)}, bf16[8,256,128]{2,1,0:T(8,128)(2,1)}) async-done(((bf16[8,256,128]{2,1,0:T(8,128)(2,1)}, bf16[8,256,128]{2,1,0:T(8,128)(2,1)}), (bf16[8,256,128]{2,1,0:T(8,128)(2,1)}, bf16[8,256,128]{2,1,0:T(8,128)(2,1)})) %all-reduce.6.cloned.1.call-update) | async-done | bytes 1048592 | tf_op jit(solution)/shard_map/psum | solution.py:9
  361.2 1.3 pad_maximum_fusion
  362.5 0.9 copy.21
  363.4 0.4 fusion.46
  363.8 0.2 copy.22
  364.0 0.1 bitcast_reduce_fusion.1
  364.1 0.2 multiply_reduce_fusion.2
  364.3 0.0 copy-done.1
  364.3 0.0 copy-done.3
  364.3 0.3 fusion.45
  364.7 0.2 multiply_reduce_fusion.1
  364.8 0.0 copy-done.2
  364.8 0.2 fusion.11
  365.1 0.7 fusion.19
  365.7 0.0 all-gather.3.cloned.1.call-update
  365.8 0.0 all-gather.5.cloned.1.call-start
  365.8 0.7 all-gather.5.cloned.1.call-update
  366.5 0.0 all-reduce.4.cloned.1.call-start
  366.6 62.6 %all-gather.3.cloned.1.call-done = bf16[256,16,128]{2,1,0:T(8,128)(2,1)} async-done(((bf16[8,16,128]{2,1,0:T(8,128)(2,1)}), bf16[256,16,128]{2,1,0:T(8,128)(2,1)}) %all-gather.3.cloned.1.call-update) | async-done | bytes 1048592 | tf_op jit(solution)/shard_map/all_gather | solution.py:59
  429.2 1.1 constant_dynamic-slice_fusion
  430.3 0.6 copy.26
  430.8 0.8 broadcast_select_fusion
  431.7 0.0 all-reduce.4.cloned.1.call-update
  431.7 0.0 copy-done.5
  431.7 0.2 fusion.3
  431.9 0.0 copy-start.4
  431.9 62.6 %all-gather.5.cloned.1.call-done = bf16[256,16,128]{2,1,0:T(8,128)(2,1)} async-done(((bf16[8,16,128]{2,1,0:T(8,128)(2,1)}), bf16[256,16,128]{2,1,0:T(8,128)(2,1)}) %all-gather.5.cloned.1.call-update) | async-done | bytes 1048592 | tf_op jit(solution)/shard_map/all_gather | solution.py:60
  494.5 7.5 %copy.24 = bf16[256,16,128]{1,0,2:T(8,128)(2,1)} copy(bf16[256,16,128]{2,1,0:T(8,128)(2,1)} %all-gather.5.cloned.1.call-done) | data formatting | bytes 2097152 | tf_op jit(solution)/shard_map/all_gather | solution.py:60
  502.1 190.6 %all-reduce.4.cloned.1.call-done = bf16[256,8,128]{0,1,2:T(8,128)(2,1)} async-done(((bf16[256,8,128]{0,1,2:T(8,128)(2,1)}), bf16[256,8,128]{0,1,2:T(8,128)(2,1)}) %all-reduce.4.cloned.1.call-update) | async-done | bytes 524304 | tf_op jit(solution)/shard_map/psum | solution.py:9
  692.7 4.8 fusion.47
  697.4 0.2 copy.25
  697.6 0.1 bitcast_reduce_fusion
  697.8 0.2 multiply_reduce_fusion
  698.0 0.0 copy-done.4
  698.0 0.8 fusion.10
  (9 shorter events, 0.1 us)
Async XLA Ops:
  6.5 2.0 copy-start
  6.5 357.8 %copy-start.1 = (bf16[8,16,128]{2,1,0:T(8,128)(2,1)S(1)}, bf16[8,16,128]{2,1,0:T(8,128)(2,1)}, u32[]{:S(2)}) copy-start(bf16[8,16,128]{2,1,0:T(8,128)(2,1)} %param.7) | copy-start | bytes 98308
  6.5 357.8 %copy-start.3 = (bf16[128,128]{1,0:T(8,128)(2,1)S(1)}, bf16[128,128]{1,0:T(8,128)(2,1)}, u32[]{:S(2)}) copy-start(bf16[128,128]{1,0:T(8,128)(2,1)} %param.10) | copy-start | bytes 98308
  6.5 358.3 %copy-start.2 = (bf16[128,512]{1,0:T(8,128)(2,1)S(1)}, bf16[128,512]{1,0:T(8,128)(2,1)}, u32[]{:S(2)}) copy-start(bf16[128,512]{1,0:T(8,128)(2,1)} %param.11) | copy-start | bytes 393220
  6.5 354.7 %all-reduce.6.cloned.1.call-start = ((), (), s32[]{:S(2)}) async-start(), calls=%async_computation.3 | async-start | bytes 2097152 | tf_op jit(solution)/shard_map/psum | solution.py:9
  66.8 364.8 %copy-start.5 = (bf16[128,128]{1,0:T(8,128)(2,1)S(1)}, bf16[128,128]{1,0:T(8,128)(2,1)}, u32[]{:S(2)}) copy-start(bf16[128,128]{1,0:T(8,128)(2,1)} %param.12) | copy-start | bytes 98308
  68.0 361.2 %all-gather.3.cloned.1.call-start = ((), (), s32[]{:S(2)}) async-start(), calls=%async_computation | async-start | bytes 1081344 | tf_op jit(solution)/shard_map/all_gather | solution.py:59
  365.8 128.8 %all-gather.5.cloned.1.call-start = ((), (), s32[]{:S(2)}) async-start(), calls=%async_computation.2 | async-start | bytes 1081344 | tf_op jit(solution)/shard_map/all_gather | solution.py:60
  366.5 326.2 %all-reduce.4.cloned.1.call-start = ((), (), s32[]{:S(2)}) async-start(), calls=%async_computation.1 | async-start | bytes 1048576 | tf_op jit(solution)/shard_map/psum | solution.py:9
  431.9 266.0 %copy-start.4 = (bf16[128,128]{1,0:T(8,128)(2,1)S(1)}, bf16[128,128]{1,0:T(8,128)(2,1)}, u32[]{:S(2)}) copy-start(bf16[128,128]{1,0:T(8,128)(2,1)} %param.13) | copy-start | bytes 98308
Sparse Core Ops, SparseCore 0:
  68.1 293.0 all-reduce.5
  365.9 63.2 all-gather.2
  431.6 62.9 all-gather.4
  497.6 195.0 all-reduce.3
where the time goes:
time: 716 us; the launch traced here: 705 us
  waiting for transfers between devices  564 us (79%)
  blocking collectives  102 us (14%)
  between operations  13.4 us (2%)
  local copies, waits for them, and re-layouts  10.9 us (2%)
  matrix products  8.68 us (1%)
    psum x2, waiting for transfers between devices, from_root(): return lax.psum(block, axis)  438 us
    all_gather x1, waiting for transfers between devices, body(): lax.all_gather(right_side, 'row', axis=0, tiled=True)  62.6 us
    all_gather x1, waiting for transfers between devices, body(): lax.all_gather(left_side, 'row', axis=0, tiled=True)  62.6 us
    all_gather x1, blocking collectives, body(): lax.all_gather(right_side, 'col', axis=1, tiled=True)  57.3 us
    all_gather x1, blocking collectives, body(): lax.all_gather(left_side, 'col', axis=1, tiled=True)  44.7 us
  transfers between devices with their start and end apart: 4, of which 4 were waited for; matrix products, arithmetic and copies ran while one was open for 2% of the time, Pallas kernels for 0%

commit v1 on v0

v1 whole, which is shorter than its diff:
```python
import functools

import jax
import jax.numpy as jnp
from jax import lax
from jax.experimental import pallas as pl
from jax.experimental.pallas import tpu as pltpu
from jax.sharding import PartitionSpec as P

MESH = pl.DeviceIdType.MESH
F32 = jnp.float32
BF16 = jnp.bfloat16


def normalize(values):
    average = jnp.mean(values, axis=-1, keepdims=True)
    centred = values - average
    spread = jnp.mean(centred * centred, axis=-1, keepdims=True)
    return centred * lax.rsqrt(spread + 1e-05)


def prepare(block, proj_ref, gate_ref):
    normed = normalize(block.astype(F32)).astype(BF16)
    projected = jnp.dot(normed, proj_ref[...], preferred_element_type=F32)
    left = jax.nn.sigmoid(projected[:, 0:128]) * projected[:, 128:256]
    right = jax.nn.sigmoid(projected[:, 256:384]) * projected[:, 384:512]
    gate = jax.nn.sigmoid(jnp.dot(normed, gate_ref[...], preferred_element_type=F32))
    return left, right, gate


def finish(block, summed, gate, final_ref):
    mixed = normalize(summed).astype(BF16)
    update = gate * jnp.dot(mixed, final_ref[...], preferred_element_type=F32)
    return (block.astype(F32) + update).astype(BF16)


def contract(left, right, sums, half):
    for i_block in range(2):
        for j_half in range(2):

            def step(chunk, total):
                a = left[chunk, half, i_block * 32 : i_block * 32 + 32, :].astype(F32)
                b = right[chunk, j_half].astype(F32)
                return total + a.reshape(4, 1, 8, 128) * b.reshape(1, 8, 8, 128)

            total = lax.fori_loop(0, 16, step, jnp.zeros((4, 8, 8, 128), F32))
            sums[half, i_block * 4 : i_block * 4 + 4, j_half * 8 : j_half * 8 + 8, :] = (
                jnp.sum(total, axis=2)
            )


def kernel(
    map_ref, proj1, gate1, final1, proj2, gate2, final2, out_ref,
    send_l1, send_r1, send_l2, send_r2, left1, right1, left2, right2, sums1, sums2, part1, part2, turned,
    out_a_l1, in_a_l1, out_b_l1, in_b_l1, out_a_r1, in_a_r1, out_b_r1, in_b_r1,
    out_a_l2, in_a_l2, out_b_l2, in_b_l2, out_a_r2, in_a_r2, out_b_r2, in_b_r2,
    out_part, in_part,
):
    row, col = lax.axis_index("row"), lax.axis_index("col")
    y, zl, core = row // 8, row // 2 % 4, row % 2
    x, zh = col // 4, col % 4

    def at(x_, y_, zh_, zl_, core_):
        return (y_ * 8 + zl_ * 2 + core_, x_ * 4 + zh_)

    def plus(value, step):
        return (value + step) % 4

    own_turn = jnp.logical_and(x == y, zh == zl)
    other_turn = jnp.logical_not(own_turn)
    sibling = at(x, y, zh, zl, 1 - core)
    pending = []

    def copy(src, dst, send, recv, device):
        return pltpu.make_async_remote_copy(
            src_ref=src, dst_ref=dst, send_sem=send, recv_sem=recv, device_id=device, device_id_type=MESH
        )

    def push(src, dst, send, recv, device):
        c = copy(src, dst, send, recv, device)
        c.start()
        pending.append(c)

    def landed(dst, recv):
        copy(dst, dst, out_part.at[0], recv, sibling).wait_recv()

    def turn_push(src, dst, send, recv, device):
        c = copy(src, dst, send, recv, device)

        @pl.when(other_turn)
        def _():
            c.start()

        @pl.when(own_turn)
        def _():
            pltpu.make_async_copy(src, dst, recv).start()

        return c

    barrier = pltpu.get_barrier_semaphore()

    def greet(device):
        pl.semaphore_signal(barrier, inc=1, device_id=device, device_id_type=MESH)

    greeted = 0
    for step in range(4):
        for side in range(2):
            c_ = (core + side) % 2
            for device in (
                at(y, x, zl, plus(zl, step), c_),
                at(y, x, plus(zh, step), zh, c_),
            ):
                if step or side:
                    greet(device)
                else:

                    @pl.when(other_turn)
                    def _(device=device):
                        greet(device)

                greeted += 1
            if step or side:
                greet(at(x, y, plus(zh, step), zl, c_))
                greeted += 1
        if step:
            greet(at(plus(x, step), y, zh, zl, core))
            greet(at(x, plus(y, step), zh, zl, core))
            greet(at(x, y, zh, plus(zl, step), core))
            greeted += 3

    block = map_ref[...].reshape(128, 128)
    left, right, gate = prepare(block, proj1, gate1)
    left, right = left.reshape(8, 2, 8, 128), right.reshape(8, 2, 8, 128)
    for side in range(2):
        send_l1[side] = left[:, side].reshape(64, 128).astype(BF16)
        send_r1[side] = right[:, side].reshape(64, 128).astype(BF16)
    mine = 4 * x + zh
    left1[mine, core] = send_l1[core]

    pl.semaphore_wait(barrier, greeted - 2 * own_turn.astype(jnp.int32))

    order = (2, 1, 3, 0)
    for step in order:
        for side in (0, 1):
            to = (core + side) % 2
            if step or side:
                push(send_l1.at[to], left1.at[mine, core], out_a_l1.at[step, side], in_a_l1.at[step, side],
                     at(x, y, plus(zh, step), zl, to))
            src, dst = send_r1.at[to], right1.at[mine, core]
            send, recv = out_a_r1.at[step, side], in_a_r1.at[zh, core]
            device = at(y, x, zl, plus(zl, step), to)
            if step or side:
                push(src, dst, send, recv, device)
            else:
                turn1 = turn_push(src, dst, send, recv, device)

    for step in (0, 1, 3, 2):
        from_zh = (zh + 4 - step) % 4
        chunk = 4 * x + from_zh
        for side in (0, 1):
            if step or side:
                landed(left1.at[chunk, (core + side) % 2], in_a_l1.at[step, side])
        for hop in (2, 1, 3):
            push(left1.at[chunk], left1.at[chunk], out_b_l1.at[hop, step], in_b_l1.at[hop, step],
                 at(plus(x, hop), y, zh, zl, core))
        chunk = 4 * y + from_zh
        for side in (0, 1):
            landed(right1.at[chunk, side], in_a_r1.at[from_zh, side])
        for hop in (2, 1, 3):
            push(right1.at[chunk], right1.at[chunk], out_b_r1.at[hop, step], in_b_r1.at[hop, from_zh],
                 at(x, plus(y, hop), zh, zl, core))
    for step in (0, 1, 3, 2):
        from_zh = (zh + 4 - step) % 4
        for hop in (1, 3, 2):
            landed(left1.at[4 * ((x + 4 - hop) % 4) + from_zh], in_b_l1.at[hop, step])
            landed(right1.at[4 * ((y + 4 - hop) % 4) + from_zh], in_b_r1.at[hop, from_zh])

    contract(left1, right1, sums1, 1 - core)
    push(sums1.at[1 - core], part1, out_part.at[0], in_part.at[0], sibling)
    contract(left1, right1, sums1, core)
    landed(part1, in_part.at[0])
    summed = (sums1[core] + part1[...]).reshape(128, 128)
    block = finish(block, summed, gate, final1)

    left, right, gate = prepare(block, proj2, gate2)
    turned[0] = left
    turned[1] = right
    for j in range(0, 16, 2):
        for which, send_ref in ((0, send_l2), (1, send_r2)):
            pair = [turned[which, pl.ds(j + k, 8, stride=16), :] for k in range(2)]
            send_ref[j // 8, (j % 8) * 8 : (j % 8) * 8 + 16, :] = jnp.concatenate(pair, axis=0).astype(BF16)
    mine = 4 * y + zl
    right2[mine] = send_r2[...]
    for step in order:
        src, dst = send_l2, left2.at[mine]
        send, recv = out_a_l2.at[step], in_a_l2.at[zl]
        device = at(y, x, plus(zh, step), zh, core)
        if step:
            push(src, dst, send, recv, device)
            push(send_r2, right2.at[mine], out_a_r2.at[step], in_a_r2.at[step], at(x, y, zh, plus(zl, step), core))
        else:
            turn2 = turn_push(src, dst, send, recv, device)

    for step in (0, 1, 3, 2):
        from_zl = (zl + 4 - step) % 4
        chunk = 4 * y + from_zl
        if step:
            landed(right2.at[chunk], in_a_r2.at[step])
        for hop in (2, 1, 3):
            push(right2.at[chunk], right2.at[chunk], out_b_r2.at[hop, step], in_b_r2.at[hop, step],
                 at(x, plus(y, hop), zh, zl, core))
        chunk = 4 * x + from_zl
        landed(left2.at[chunk], in_a_l2.at[from_zl])
        for hop in (2, 1, 3):
            push(left2.at[chunk], left2.at[chunk], out_b_l2.at[hop, step], in_b_l2.at[hop, from_zl],
                 at(plus(x, hop), y, zh, zl, core))
    for step in (0, 1, 3, 2):
        from_zl = (zl + 4 - step) % 4
        for hop in (1, 3, 2):
            landed(right2.at[4 * ((y + 4 - hop) % 4) + from_zl], in_b_r2.at[hop, step])
            landed(left2.at[4 * ((x + 4 - hop) % 4) + from_zl], in_b_l2.at[hop, from_zl])

    contract(left2, right2, sums2, 1 - core)
    push(sums2.at[1 - core], part2, out_part.at[1], in_part.at[1], sibling)
    contract(left2, right2, sums2, core)
    landed(part2, in_part.at[1])
    summed = (sums2[core] + part2[...]).reshape(128, 128)
    out_ref[...] = finish(block, summed, gate, final2).reshape(8, 16, 128)

    for c in pending:
        c.wait_send()

    @pl.when(other_turn)
    def _():
        turn1.wait_send()
        turn2.wait_send()


def body(*args):
    vmem = pl.BlockSpec(memory_space=pltpu.VMEM)
    dma = pltpu.SemaphoreType.DMA
    half = pltpu.VMEM((2, 64, 128), BF16)
    gathered = pltpu.VMEM((16, 2, 64, 128), BF16)
    return pl.pallas_call(
        kernel,
        out_shape=jax.ShapeDtypeStruct((8, 16, 128), BF16),
        in_specs=[vmem] * 7,
        out_specs=vmem,
        scratch_shapes=[half] * 4
        + [gathered] * 4
        + [pltpu.VMEM((2, 8, 16, 128), F32)] * 2
        + [pltpu.VMEM((8, 16, 128), F32)] * 2
        + [pltpu.VMEM((2, 128, 128), F32)]
        + [dma((4, 2))] * 2 + [dma((4, 4))] * 2
        + [dma((4, 2))] * 2 + [dma((4, 4))] * 2
        + [dma((4,))] * 2 + [dma((4, 4))] * 2
        + [dma((4,))] * 2 + [dma((4, 4))] * 2
        + [dma((2,))] * 2,
        compiler_params=pltpu.CompilerParams(
            collective_id=0, has_side_effects=True, vmem_limit_bytes=32 * 1024 * 1024
        ),
        name="triangles",
    )(*args)


def solution(mesh):
    return jax.shard_map(
        body,
        mesh=mesh,
        in_specs=(P("row", "col", None), P(), P(), P(), P(), P(), P()),
        out_specs=P("row", "col", None),
        check_vma=False,
    )
```

time: 716 us -> 76.6 us (0.11); the launches traced: 705 us -> 76.1 us
  waiting for transfers between devices: 564 us -> 0 us
  blocking collectives: 102 us -> 0 us
  Pallas kernels: 0 us -> 69.8 us
  between operations: 13.4 us -> 0.02 us
  matrix products: 8.68 us -> 0 us
    psum x2 -> x0, waiting for transfers between devices: 438 us -> none  [from_root(): return lax.psum(block, axis)]
    all_gather x2 -> x0, waiting for transfers between devices: 125 us -> none  [the longest x1 62.6 us: body(): lax.all_gather(right_side, 'row', axis=0, tiled=True)]
    all_gather x2 -> x0, blocking collectives: 102 us -> none  [the longest x1 57.3 us: body(): lax.all_gather(right_side, 'col', axis=1, tiled=True)]
    pallas_call x0 -> x1, Pallas kernels: none -> 69.8 us  [body(): pl.pallas_call(kernel, out_shape=jax.ShapeDtypeStruct((8, 16, 128), BF16)...]
    dot_general x8 -> x0, matrix products: 8.68 us -> none  [the longest x1 4.75 us: body(): lax.dot_general(left_cols, right_cols, (((0,), (0,)), ((2,), (2,))), pref...]
    all_gather x2 -> x0, local copies, waits for them, and re-layouts: 7.94 us -> none  [the longest x1 7.55 us: body(): lax.all_gather(right_side, 'row', axis=0, tiled=True)]
  transfers between devices with their start and end apart: 4 -> 0, of which waited for: 4 -> 0; matrix products, arithmetic and copies ran while one was open for 2% -> 0% of each run, Pallas kernels for 0% -> 0%
where the time goes in v1:
time: 76.6 us; the launch traced here: 76.1 us
  Pallas kernels  69.8 us (91%)
  local copies, waits for them, and re-layouts  6.21 us (8%)
    pallas_call x1, Pallas kernels, body(): pl.pallas_call(kernel, out_shape=jax.ShapeDtypeStruct((8, 16, 128), BF16)...  69.8 us
    unnamed x15, local copies, waits for them, and re-layouts  6.21 us

profile of v1, /device:TPU:1, one launch (start us, length us, event | category | flops | bytes accessed | tf_op | source)
XLA Modules:
  0.0 76.1 jit_solution(3373797933834499399)
XLA Ops:
  0.0 0.0 copy-start
  0.0 0.9 %copy-done = bf16[128,512]{1,0:T(8,128)(2,1)S(1)} copy-done((bf16[128,512]{1,0:T(8,128)(2,1)S(1)}, bf16[128,512]{1,0:T(8,128)(2,1)}, u32[]{:S(2)}) %copy-start) | copy-done | bytes 131096
  0.9 0.0 copy-start.1
  0.9 0.9 %copy-done.1 = bf16[128,512]{1,0:T(8,128)(2,1)S(1)} copy-done((bf16[128,512]{1,0:T(8,128)(2,1)S(1)}, bf16[128,512]{1,0:T(8,128)(2,1)}, u32[]{:S(2)}) %copy-start.1) | copy-done | bytes 131096
  1.8 0.0 copy-start.2
  1.8 0.8 copy-done.2
  2.6 0.0 copy-start.3
  2.6 0.8 copy-done.3
  3.3 0.0 copy-start.4
  3.3 0.8 copy-done.4
  4.1 0.0 copy-start.5
  4.1 0.8 copy-done.5
  4.8 0.0 copy-start.6
  4.8 0.8 copy-done.6
  5.6 69.8 %triangles.1 = bf16[8,16,128]{2,1,0:T(8,128)(2,1)S(1)} custom-call(bf16[8,16,128]{2,1,0:T(8,128)(2,1)S(1)} %copy-done.2, bf16[128,512]{1,0:T(8,128)(2,1)S(1)} %copy-done, bf16[128,128]{1,0:T(8,128)(2,1)S(1)} %copy-done.3, bf16[128,128]{1,0:T(8,128)(2,1)S(1)} %copy-done.4, bf16[128,512]{1,0:T(8,128)(2,1)S(1)} %copy-done.1, bf16[128,128]{1,0:T(8,128)(2,1)S(1)} %copy-done.5, ...), custom_call_target="tpu_custom_call" | custom-call | tf_op jit(solution)/shard_map/triangles/pallas_call | solution.py:244
  75.5 0.6 copy.9
Async XLA Ops:
  0.0 0.9 %copy-start = (bf16[128,512]{1,0:T(8,128)(2,1)S(1)}, bf16[128,512]{1,0:T(8,128)(2,1)}, u32[]{:S(2)}) copy-start(bf16[128,512]{1,0:T(8,128)(2,1)} %proj1.1) | copy-start | bytes 393220
  0.9 0.9 %copy-start.1 = (bf16[128,512]{1,0:T(8,128)(2,1)S(1)}, bf16[128,512]{1,0:T(8,128)(2,1)}, u32[]{:S(2)}) copy-start(bf16[128,512]{1,0:T(8,128)(2,1)} %proj2.1) | copy-start | bytes 393220
  1.8 0.8 copy-start.2
  2.6 0.8 copy-start.3
  3.3 0.8 copy-start.4
  4.1 0.8 copy-start.5
  4.8 0.8 copy-start.6

commit v2 on v0

v2 whole, which is shorter than its diff:
```python
import jax
import jax.numpy as jnp
from jax import lax
from jax.experimental import pallas as pl
from jax.experimental.pallas import tpu as pltpu
from jax.sharding import PartitionSpec as P

MESH = pl.DeviceIdType.MESH
F32 = jnp.float32
BF16 = jnp.bfloat16


def normalize(values):
    average = jnp.mean(values, axis=-1, keepdims=True)
    centred = values - average
    spread = jnp.mean(centred * centred, axis=-1, keepdims=True)
    return centred * lax.rsqrt(spread + 1e-05)


def prepare(block, proj_ref):
    normed = normalize(block.astype(F32)).astype(BF16)
    projected = jnp.dot(normed, proj_ref[...], preferred_element_type=F32)
    left = jax.nn.sigmoid(projected[:, 0:128]) * projected[:, 128:256]
    right = jax.nn.sigmoid(projected[:, 256:384]) * projected[:, 384:512]
    return left, right


def output_gate(block, gate_ref):
    normed = normalize(block.astype(F32)).astype(BF16)
    return jax.nn.sigmoid(jnp.dot(normed, gate_ref[...], preferred_element_type=F32))


def finish(block, summed, gate, final_ref):
    mixed = normalize(summed).astype(BF16)
    update = gate * jnp.dot(mixed, final_ref[...], preferred_element_type=F32)
    return (block.astype(F32) + update).astype(BF16)


def outer(a, b):
    a, b = a.astype(F32), b.astype(F32)
    i, j, k = 4, 8, a.shape[0] // 32
    a, b = a.reshape(i, k, 8, 128), b.reshape(j, k, 8, 128)
    total = None
    for n in range(k):
        term = a[:, None, n] * b[None, :, n]
        total = term if total is None else total + term
    return total


def kernel(
    map_in, proj1_in, gate1_in, final1_in, proj2_in, gate2_in, final2_in, out_ref,
    map_ref, proj1, gate1, final1, proj2, gate2, final2, load,
    send_l1, send_r1, left1, right1, send_p1, part1, own1, block1, middle,
    turned, send_l2, send_r2, left2, right2, total2, sums2, part2, block2,
    out_l1, in_l1, out_a_r1, in_a_r1, out_b_r1, in_b_r1, out_p1, in_p1, out_z, in_z,
    out_a_l2, in_a_l2, out_b_l2, in_b_l2, out_a_r2, in_a_r2, out_b_r2, in_b_r2, out_p2, in_p2,
):
    row, col = lax.axis_index("row"), lax.axis_index("col")
    y, zl, core = row // 8, row // 2 % 4, row % 2
    x, zh = col // 4, col % 4

    def at(x_, y_, zh_, zl_, core_):
        return (y_ * 8 + zl_ * 2 + core_, x_ * 4 + zh_)

    def plus(value, step):
        return (value + step) % 4

    def minus(value, step):
        return (value + 4 - step) % 4

    flat, level = x == y, zl == zh
    sibling = at(x, y, zh, zl, 1 - core)
    swapped = at(y, x, zh, zl, core)
    pending, turns = [], []

    def copy(src, dst, send, recv, device):
        return pltpu.make_async_remote_copy(
            src_ref=src, dst_ref=dst, send_sem=send, recv_sem=recv, device_id=device, device_id_type=MESH
        )

    def push(src, dst, send, recv, device):
        c = copy(src, dst, send, recv, device)
        c.start()
        pending.append(c)

    def push_unless(stays, src, dst, send, recv, device):
        c = copy(src, dst, send, recv, device)

        @pl.when(jnp.logical_not(stays))
        def _():
            c.start()

        @pl.when(stays)
        def _():
            pltpu.make_async_copy(src, dst, recv).start()

        turns.append((stays, c))

    def landed(dst, recv):
        copy(dst, dst, out_p2.at[0], recv, sibling).wait_recv()

    loads = [
        pltpu.make_async_copy(src, dst, load.at[n])
        for n, (src, dst) in enumerate((
            (map_in, map_ref), (proj1_in, proj1), (gate1_in, gate1), (final1_in, final1),
            (proj2_in, proj2), (gate2_in, gate2), (final2_in, final2),
        ))
    ]
    for c in loads:
        c.start()

    barrier = pltpu.get_barrier_semaphore()
    greeted = []

    def greet(device, stays=None):
        def signal():
            pl.semaphore_signal(barrier, inc=1, device_id=device, device_id_type=MESH)

        if stays is None:
            signal()
            greeted.append(1)
        else:
            pl.when(jnp.logical_not(stays))(signal)
            greeted.append(1 - stays.astype(jnp.int32))

    for step in (2, 1, 3, 0):
        for side in (0, 1):
            other = (core + side) % 2
            home = None if step or side else flat
            if step or side:
                greet(at(x, y, plus(zh, step), zl, other))
            greet(at(y, plus(y, step), zh, zl, other), home)
            greet(at(plus(x, step), x, zh, zl, other), home)
        home = None if step else level
        greet(at(x, y, plus(zh, step), zh, core), home)
        greet(at(x, y, zl, plus(zl, step), core), home)
        greet(at(y, x, zh, plus(zl, step), core), None if step else flat)
        if step:
            greet(at(plus(x, step), y, zh, zl, core))
            greet(at(x, plus(y, step), zh, zl, core))
            greet(at(x, y, zh, plus(zl, step), core))

    for c in loads[:2]:
        c.wait()
    left, right = prepare(map_ref[...].reshape(128, 128), proj1)
    send_r1[...] = right.astype(BF16)
    right1[x, zl] = send_r1[...]
    send_l1[...] = left.astype(BF16)

    pl.semaphore_wait(barrier, sum(greeted))

    for step in (2, 1, 3):
        push(send_r1, right1.at[x, zl], out_a_r1.at[step], in_a_r1.at[zl], at(x, y, zh, plus(zl, step), core))
    for step in (2, 1, 3, 0):
        for side in (1, 0):
            device = at(y, plus(y, step), zh, zl, (core + side) % 2)
            args = send_l1, left1.at[x, core], out_l1.at[step, side], in_l1.at[x, core], device
            if step or side:
                push(*args)
            else:
                push_unless(flat, *args)
    for step in (0, 1, 3, 2):
        from_zl = minus(zl, step)
        piece = right1.at[x, from_zl]
        if step:
            landed(piece, in_a_r1.at[from_zl])
        for hop in (2, 1, 3):
            push(piece, piece, out_b_r1.at[hop, step], in_b_r1.at[x, from_zl], at(plus(x, hop), y, zh, zl, core))
    push_unless(flat, map_ref, block1, out_z.at[0], in_z.at[0], swapped)

    for from_x in range(4):
        for side in range(2):
            landed(left1.at[from_x, side], in_l1.at[from_x, side])
    for step in (2, 1, 3, 0):
        to_zh = plus(zh, step)
        for hop in (1, 3, 2):
            landed(right1.at[minus(x, hop), to_zh], in_b_r1.at[minus(x, hop), to_zh])

        def four_rows(n, _, step=step, to_zh=to_zh):
            half, quarter = n // 2, n % 2
            total = None
            for from_x in range(4):
                term = outer(
                    left1[from_x, half, pl.ds(pl.multiple_of(quarter * 64, 64), 64), :], right1[from_x, to_zh]
                )
                total = term if total is None else total + term
            part = jnp.sum(total, axis=2).reshape(32, 128)
            rows = pl.ds(pl.multiple_of(quarter * 32, 32), 32)
            send_p1[step, half, rows, :] = part.astype(BF16)
            if step == 0:
                own1[half, rows, :] = part
            return 0

        lax.fori_loop(0, 4, four_rows, 0)
        for side in (0, 1):
            to = (core + side) % 2
            if step or side:
                push(send_p1.at[step, to], part1.at[step, core], out_p1.at[step, side], in_p1.at[step, core],
                     at(x, y, to_zh, zl, to))

    landed(block1, in_z.at[0])
    for c in loads[2:]:
        c.wait()
    block = block1[...].reshape(128, 128)
    gate = output_gate(block, gate1)
    landed(part1.at[0, 1 - core], in_p1.at[0, 1 - core])
    for step in (1, 3, 2):
        for side in (0, 1):
            landed(part1.at[step, side], in_p1.at[step, side])
    halves = []
    for side in range(2):
        near = jnp.where(core == side, own1[side], part1[0, side].astype(F32))
        rest = part1[1, side].astype(F32) + part1[2, side].astype(F32) + part1[3, side].astype(F32)
        halves.append((near + rest).reshape(8, 1, 8, 128))
    summed = jnp.concatenate(halves, axis=1).reshape(128, 128)
    block = finish(block, summed, gate, final1)
    middle[...] = block.reshape(8, 16, 128)

    left, right = prepare(block, proj2)
    turned[0] = left
    turned[1] = right
    for which, send_ref in ((0, send_l2), (1, send_r2)):
        for j in range(0, 16, 2):
            pair = [turned[which, pl.ds(j + k, 8, stride=16), :] for k in range(2)]
            send_ref[j // 8, (j % 8) * 8 : (j % 8) * 8 + 16, :] = jnp.concatenate(pair, axis=0).astype(BF16)
    for step in (2, 1, 3, 0):
        args = send_l2, left2.at[x, zl], out_a_l2.at[step], in_a_l2.at[zl], at(x, y, plus(zh, step), zh, core)
        if step:
            push(*args)
        else:
            push_unless(level, *args)
        args = send_r2, right2.at[x, zl], out_a_r2.at[step], in_a_r2.at[zl], at(y, x, zh, plus(zl, step), core)
        if step:
            push(*args)
        else:
            push_unless(flat, *args)
    push_unless(flat, middle, block2, out_z.at[1], in_z.at[1], swapped)

    for step in (0, 1, 3, 2):
        from_zl = minus(zl, step)
        piece = right2.at[y, from_zl]
        landed(piece, in_a_r2.at[from_zl])
        for hop in (2, 1, 3):
            push(piece, piece, out_b_r2.at[hop, step], in_b_r2.at[y, from_zl], at(x, plus(y, hop), zh, zl, core))
        piece = left2.at[x, from_zl]
        landed(piece, in_a_l2.at[from_zl])
        for hop in (2, 1, 3):
            push(piece, piece, out_b_l2.at[hop, step], in_b_l2.at[x, from_zl], at(plus(x, hop), y, zh, zl, core))

    landed(block2, in_z.at[1])
    block = block2[...].reshape(128, 128)
    gate = output_gate(block, gate2)
    for step in (0, 1, 3, 2):
        from_zl = minus(zl, step)
        for hop in (1, 3, 2):
            landed(right2.at[minus(y, hop), from_zl], in_b_r2.at[minus(y, hop), from_zl])
            landed(left2.at[minus(x, hop), from_zl], in_b_l2.at[minus(x, hop), from_zl])

        def four_by_eight(n, _, step=step, from_zl=from_zl):
            half, quarter, j_half = n // 4, n // 2 % 2, n % 2
            total = None if step == 0 else total2[n]
            for from_x in range(4):
                term = outer(
                    left2[from_x, from_zl, half, pl.ds(pl.multiple_of(quarter * 32, 32), 32), :],
                    right2[from_x, from_zl, j_half],
                )
                total = term if total is None else total + term
            if step == 2:
                sums2[half, quarter, :, j_half] = jnp.sum(total, axis=2)
            else:
                total2[n] = total
            return 0

        if step == 2:
            first = (1 - core) * 4
            lax.fori_loop(first, first + 4, four_by_eight, 0)
            push(sums2.at[1 - core], part2, out_p2.at[0], in_p2.at[0], sibling)
            first = core * 4
            lax.fori_loop(first, first + 4, four_by_eight, 0)
        else:
            lax.fori_loop(0, 8, four_by_eight, 0)

    landed(part2, in_p2.at[0])
    summed = (sums2[core] + part2[...]).reshape(128, 128)
    out_ref[...] = finish(block, summed, gate, final2).reshape(8, 16, 128)

    for c in pending:
        c.wait_send()
    for stays, c in turns:
        pl.when(jnp.logical_not(stays))(c.wait_send)


def body(*args):
    dma = pltpu.SemaphoreType.DMA
    weights = [pltpu.VMEM((128, 512), BF16), pltpu.VMEM((128, 128), BF16), pltpu.VMEM((128, 128), BF16)]
    tile = pltpu.VMEM((8, 16, 128), BF16)
    return pl.pallas_call(
        kernel,
        out_shape=jax.ShapeDtypeStruct((8, 16, 128), BF16),
        in_specs=[pl.BlockSpec(memory_space=pl.ANY)] * 7,
        out_specs=pl.BlockSpec(memory_space=pltpu.VMEM),
        scratch_shapes=[tile, *weights, *weights, dma((7,))]
        + [pltpu.VMEM((128, 128), BF16)] * 2
        + [pltpu.VMEM((4, 2, 128, 128), BF16), pltpu.VMEM((4, 4, 128, 128), BF16)]
        + [pltpu.VMEM((4, 2, 64, 128), BF16)] * 2
        + [pltpu.VMEM((2, 64, 128), F32), tile, tile]
        + [pltpu.VMEM((2, 128, 128), F32)]
        + [pltpu.VMEM((2, 64, 128), BF16)] * 2
        + [pltpu.VMEM((4, 4, 2, 64, 128), BF16)] * 2
        + [pltpu.VMEM((8, 4, 8, 8, 128), F32), pltpu.VMEM((2, 2, 4, 2, 8, 128), F32)]
        + [pltpu.VMEM((2, 4, 2, 8, 128), F32), tile]
        + [dma((4, 2))] * 2 + [dma((4,))] * 2 + [dma((4, 4))] * 2 + [dma((4, 2))] * 2 + [dma((2,))] * 2
        + [dma((4,))] * 2 + [dma((4, 4))] * 2 + [dma((4,))] * 2 + [dma((4, 4))] * 2 + [dma((1,))] * 2,
        compiler_params=pltpu.CompilerParams(
            collective_id=0, has_side_effects=True, vmem_limit_bytes=64 * 1024 * 1024 - 65536
        ),
        name="triangles",
    )(*args)


def solution(mesh):
    return jax.shard_map(
        body,
        mesh=mesh,
        in_specs=(P("row", "col", None), P(), P(), P(), P(), P(), P()),
        out_specs=P("row", "col", None),
        check_vma=False,
    )
```

time: 716 us -> 67.9 us (0.09)
  the two profiles are of different devices: /device:TPU:1 before, /device:TPU:3 now
where the time goes in v2:
time: 67.9 us; the launch traced here: 67.7 us
  Pallas kernels  66.3 us (98%)
  local copies, waits for them, and re-layouts  1.38 us (2%)
    pallas_call x1, Pallas kernels, body(): pl.pallas_call(kernel, out_shape=jax.ShapeDtypeStruct((8, 16, 128), BF16)...  66.3 us
    unnamed x1, local copies, waits for them, and re-layouts  1.38 us

profile of v2, /device:TPU:3, one launch (start us, length us, event | category | flops | bytes accessed | tf_op | source)
XLA Modules:
  0.0 67.7 jit_solution(16865221580525974343)
XLA Ops:
  0.0 66.3 %triangles.1 = bf16[8,16,128]{2,1,0:T(8,128)(2,1)} custom-call(bf16[8,16,128]{2,1,0:T(8,128)(2,1)} %map_in.1, bf16[128,512]{1,0:T(8,128)(2,1)} %proj1_in.1, bf16[128,128]{1,0:T(8,128)(2,1)} %gate1_in.1, bf16[128,128]{1,0:T(8,128)(2,1)} %final1_in.1, bf16[128,512]{1,0:T(8,128)(2,1)} %proj2_in.1, bf16[128,128]{1,0:T(8,128)(2,1)} %gate2_in.1, ...), custom_call_target="tpu_custom_call" | custom-call | tf_op jit(solution)/shard_map/triangles/pallas_call | solution.py:297
  66.3 1.4 %copy.9 = bf16[8,16,128]{2,1,0:T(8,128)(2,1)} copy(bf16[8,16,128]{2,1,0:T(8,128)(2,1)} %triangles.1) | data formatting | bytes 65536

commit v3 on v2

--- a/solution.py
+++ b/solution.py
@@ -51,9 +51,9 @@
     map_in, proj1_in, gate1_in, final1_in, proj2_in, gate2_in, final2_in, out_ref,
     map_ref, proj1, gate1, final1, proj2, gate2, final2, load,
     send_l1, send_r1, left1, right1, send_p1, part1, own1, block1, middle,
-    turned, send_l2, send_r2, left2, right2, total2, sums2, part2, block2,
+    turned, send_l2, send_r2, left2, right2, send_p2, part2, block2,
     out_l1, in_l1, out_a_r1, in_a_r1, out_b_r1, in_b_r1, out_p1, in_p1, out_z, in_z,
-    out_a_l2, in_a_l2, out_b_l2, in_b_l2, out_a_r2, in_a_r2, out_b_r2, in_b_r2, out_p2, in_p2,
+    out_a_l2, in_a_l2, out_b_l2, in_b_l2, out_r2, in_r2, out_p2, in_p2, out_t, in_t, far,
 ):
     row, col = lax.axis_index("row"), lax.axis_index("col")
     y, zl, core = row // 8, row // 2 % 4, row % 2
@@ -68,7 +68,7 @@
     def minus(value, step):
         return (value + 4 - step) % 4
 
-    flat, level = x == y, zl == zh
+    flat = x == y
     sibling = at(x, y, zh, zl, 1 - core)
     swapped = at(y, x, zh, zl, core)
     pending, turns = [], []
@@ -123,22 +123,16 @@
             pl.when(jnp.logical_not(stays))(signal)
             greeted.append(1 - stays.astype(jnp.int32))
 
-    for step in (2, 1, 3, 0):
+    for step in (2, 1, 3):
         for side in (0, 1):
             other = (core + side) % 2
-            home = None if step or side else flat
-            if step or side:
+            if step != 2:
                 greet(at(x, y, plus(zh, step), zl, other))
-            greet(at(y, plus(y, step), zh, zl, other), home)
-            greet(at(plus(x, step), x, zh, zl, other), home)
-        home = None if step else level
-        greet(at(x, y, plus(zh, step), zh, core), home)
-        greet(at(x, y, zl, plus(zl, step), core), home)
-        greet(at(y, x, zh, plus(zl, step), core), None if step else flat)
-        if step:
-            greet(at(plus(x, step), y, zh, zl, core))
-            greet(at(x, plus(y, step), zh, zl, core))
-            greet(at(x, y, zh, plus(zl, step), core))
+            greet(at(x, plus(y, step), zh, zl, other))
+        greet(at(plus(x, step), y, zh, zl, core))
+        greet(at(x, y, zh, plus(zl, step), core))
+    greet(sibling)
+    greet(swapped, flat)
 
     for c in loads[:2]:
         c.wait()
@@ -149,28 +143,46 @@
 
     pl.semaphore_wait(barrier, sum(greeted))
 
+    for step in (1, 3):
+        pl.semaphore_signal(far, inc=1, device_id=at(x, y, plus(zh, step), zl, core), device_id_type=MESH)
+    push_unless(flat, send_l1, left1.at[x, core], out_t.at[0], in_t.at[0], swapped)
     for step in (2, 1, 3):
         push(send_r1, right1.at[x, zl], out_a_r1.at[step], in_a_r1.at[zl], at(x, y, zh, plus(zl, step), core))
+
+    def right_over_x(from_zl, n):
+        piece = right1.at[x, from_zl]
+        return [
+            copy(piece, piece, out_b_r1.at[hop, n], in_b_r1.at[x, from_zl], at(plus(x, hop), y, zh, zl, core))
+            for hop in (2, 1, 3)
+        ]
+
+    for c in right_over_x(zl, 4):
+        c.start()
+        pending.append(c)
+    push_unless(flat, map_ref, block1, out_z.at[0], in_z.at[0], swapped)
+    landed(left1.at[y, core], in_t.at[0])
     for step in (2, 1, 3, 0):
         for side in (1, 0):
-            device = at(y, plus(y, step), zh, zl, (core + side) % 2)
-            args = send_l1, left1.at[x, core], out_l1.at[step, side], in_l1.at[x, core], device
-            if step or side:
-                push(*args)
-            else:
-                push_unless(flat, *args)
+            if step or side:
+                push(left1.at[y, core], left1.at[y, core], out_l1.at[step, side], in_l1.at[y, core],
+                     at(x, plus(y, step), zh, zl, (core + side) % 2))
+    for step in (2, 1, 3, 0):
+        from_zl = plus(zh, step)
+        copies = right_over_x(from_zl, step)
+
+        @pl.when(from_zl != zl)
+        def _(from_zl=from_zl, copies=copies):
+            landed(right1.at[x, from_zl], in_a_r1.at[from_zl])
+            for c in copies:
+                c.start()
+
+        turns.extend((from_zl == zl, c) for c in copies)
+
     for step in (0, 1, 3, 2):
-        from_zl = minus(zl, step)
-        piece = right1.at[x, from_zl]
-        if step:
-            landed(piece, in_a_r1.at[from_zl])
-        for hop in (2, 1, 3):
-            push(piece, piece, out_b_r1.at[hop, step], in_b_r1.at[x, from_zl], at(plus(x, hop), y, zh, zl, core))
-    push_unless(flat, map_ref, block1, out_z.at[0], in_z.at[0], swapped)
-
-    for from_x in range(4):
-        for side in range(2):
-            landed(left1.at[from_x, side], in_l1.at[from_x, side])
+        for side in (0, 1):
+            if step or side:
+                from_, other = minus(y, step), (core + side) % 2
+                landed(left1.at[from_, other], in_l1.at[from_, other])
     for step in (2, 1, 3, 0):
         to_zh = plus(zh, step)
         for hop in (1, 3, 2):
@@ -192,6 +204,8 @@
             return 0
 
         lax.fori_loop(0, 4, four_rows, 0)
+        if step == 2:
+            pl.semaphore_wait(far, 2)
         for side in (0, 1):
             to = (core + side) % 2
             if step or side:
@@ -223,65 +237,73 @@
         for j in range(0, 16, 2):
             pair = [turned[which, pl.ds(j + k, 8, stride=16), :] for k in range(2)]
             send_ref[j // 8, (j % 8) * 8 : (j % 8) * 8 + 16, :] = jnp.concatenate(pair, axis=0).astype(BF16)
-    for step in (2, 1, 3, 0):
-        args = send_l2, left2.at[x, zl], out_a_l2.at[step], in_a_l2.at[zl], at(x, y, plus(zh, step), zh, core)
-        if step:
-            push(*args)
-        else:
-            push_unless(level, *args)
-        args = send_r2, right2.at[x, zl], out_a_r2.at[step], in_a_r2.at[zl], at(y, x, zh, plus(zl, step), core)
-        if step:
-            push(*args)
-        else:
-            push_unless(flat, *args)
+    left2[x, zh, core] = send_l2[core]
+    for step in (2, 1, 3, 0):
+        for side in (0, 1):
+            to = (core + side) % 2
+            if step or side:
+                push(send_l2.at[to], left2.at[x, zh, core], out_a_l2.at[step, side], in_a_l2.at[zh, core],
+                     at(x, y, plus(zh, step), zl, to))
+    push_unless(flat, send_r2, right2.at[x, core], out_t.at[1], in_t.at[1], swapped)
     push_unless(flat, middle, block2, out_z.at[1], in_z.at[1], swapped)
 
-    for step in (0, 1, 3, 2):
-        from_zl = minus(zl, step)
-        piece = right2.at[y, from_zl]
-        landed(piece, in_a_r2.at[from_zl])
+    def left_over_x(step):
+        from_zh = minus(zh, step)
+        for side in (0, 1):
+            if step or side:
+                other = (core + side) % 2
+                landed(left2.at[x, from_zh, other], in_a_l2.at[from_zh, other])
+        piece = left2.at[x, from_zh]
         for hop in (2, 1, 3):
-            push(piece, piece, out_b_r2.at[hop, step], in_b_r2.at[y, from_zl], at(x, plus(y, hop), zh, zl, core))
-        piece = left2.at[x, from_zl]
-        landed(piece, in_a_l2.at[from_zl])
-        for hop in (2, 1, 3):
-            push(piece, piece, out_b_l2.at[hop, step], in_b_l2.at[x, from_zl], at(plus(x, hop), y, zh, zl, core))
-
+            push(piece, piece, out_b_l2.at[hop, step], in_b_l2.at[x, from_zh], at(plus(x, hop), y, zh, zl, core))
+
+    left_over_x(0)
+    landed(right2.at[y, core], in_t.at[1])
+    for step in (2, 1, 3, 0):
+        for side in (1, 0):
+            if step or side:
+                push(right2.at[y, core], right2.at[y, core], out_r2.at[step, side], in_r2.at[y, core],
+                     at(x, plus(y, step), zh, zl, (core + side) % 2))
+    left_over_x(1)
+    left_over_x(3)
     landed(block2, in_z.at[1])
     block = block2[...].reshape(128, 128)
     gate = output_gate(block, gate2)
     for step in (0, 1, 3, 2):
-        from_zl = minus(zl, step)
+        for side in (0, 1):
+            if step or side:
+                from_, other = minus(y, step), (core + side) % 2
+                landed(right2.at[from_, other], in_r2.at[from_, other])
+    left_over_x(2)
+
+    for step in (0, 1, 3, 2):
+        from_zh = minus(zh, step)
         for hop in (1, 3, 2):
-            landed(right2.at[minus(y, hop), from_zl], in_b_r2.at[minus(y, hop), from_zl])
-            landed(left2.at[minus(x, hop), from_zl], in_b_l2.at[minus(x, hop), from_zl])
-
-        def four_by_eight(n, _, step=step, from_zl=from_zl):
-            half, quarter, j_half = n // 4, n // 2 % 2, n % 2
-            total = None if step == 0 else total2[n]
-            for from_x in range(4):
-                term = outer(
-                    left2[from_x, from_zl, half, pl.ds(pl.multiple_of(quarter * 32, 32), 32), :],
-                    right2[from_x, from_zl, j_half],
-                )
-                total = term if total is None else total + term
-            if step == 2:
-                sums2[half, quarter, :, j_half] = jnp.sum(total, axis=2)
-            else:
-                total2[n] = total
+            landed(left2.at[minus(x, hop), from_zh], in_b_l2.at[minus(x, hop), from_zh])
+
+        def four_rows2(quarter, _, step=step, from_zh=from_zh):
+            parts = []
+            for j_half in range(2):
+                total = None
+                for from_x in range(4):
+                    for other in range(2):
+                        term = outer(
+                            left2[from_x, from_zh, other, pl.ds(pl.multiple_of(quarter * 32, 32), 32), :],
+                            right2[from_x, other, j_half],
+                        )
+                        total = term if total is None else total + term
+                parts.append(jnp.sum(total, axis=2).reshape(4, 1, 8, 128))
+            send_p2[step, quarter] = jnp.concatenate(parts, axis=1).reshape(64, 128).astype(BF16)
             return 0
 
-        if step == 2:
-            first = (1 - core) * 4
-            lax.fori_loop(first, first + 4, four_by_eight, 0)
-            push(sums2.at[1 - core], part2, out_p2.at[0], in_p2.at[0], sibling)
-            first = core * 4
-            lax.fori_loop(first, first + 4, four_by_eight, 0)
-        else:
-            lax.fori_loop(0, 8, four_by_eight, 0)
-
-    landed(part2, in_p2.at[0])
-    summed = (sums2[core] + part2[...]).reshape(128, 128)
+        lax.fori_loop(0, 2, four_rows2, 0)
+        push_unless(from_zh == zl, send_p2.at[step], part2.at[zl], out_p2.at[step], in_p2.at[zl],
+                    at(x, y, zh, from_zh, core))
+
+    for from_zl in range(4):
+        landed(part2.at[from_zl], in_p2.at[from_zl])
+    summed = [part2[n].astype(F32).reshape(128, 128) for n in range(4)]
+    summed = (summed[0] + summed[1]) + (summed[2] + summed[3])
     out_ref[...] = finish(block, summed, gate, final2).reshape(8, 16, 128)
 
     for c in pending:
@@ -306,11 +328,12 @@
         + [pltpu.VMEM((2, 64, 128), F32), tile, tile]
         + [pltpu.VMEM((2, 128, 128), F32)]
         + [pltpu.VMEM((2, 64, 128), BF16)] * 2
-        + [pltpu.VMEM((4, 4, 2, 64, 128), BF16)] * 2
-        + [pltpu.VMEM((8, 4, 8, 8, 128), F32), pltpu.VMEM((2, 2, 4, 2, 8, 128), F32)]
-        + [pltpu.VMEM((2, 4, 2, 8, 128), F32), tile]
-        + [dma((4, 2))] * 2 + [dma((4,))] * 2 + [dma((4, 4))] * 2 + [dma((4, 2))] * 2 + [dma((2,))] * 2
-        + [dma((4,))] * 2 + [dma((4, 4))] * 2 + [dma((4,))] * 2 + [dma((4, 4))] * 2 + [dma((1,))] * 2,
+        + [pltpu.VMEM((4, 4, 2, 64, 128), BF16), pltpu.VMEM((4, 2, 2, 64, 128), BF16)]
+        + [pltpu.VMEM((4, 2, 64, 128), BF16)] * 2
+        + [tile]
+        + [dma((4, 2))] * 2 + [dma((4,))] * 2 + [dma((4, 5)), dma((4, 4))] + [dma((4, 2))] * 2 + [dma((2,))] * 2
+        + [dma((4, 2))] * 2 + [dma((4, 4))] * 2 + [dma((4, 2))] * 2 + [dma((4,))] * 2 + [dma((2,))] * 2
+        + [pltpu.SemaphoreType.REGULAR],
         compiler_params=pltpu.CompilerParams(
             collective_id=0, has_side_effects=True, vmem_limit_bytes=64 * 1024 * 1024 - 65536
         ),

time: 67.9 us -> 56 us (0.82)
  the two profiles are of different devices: /device:TPU:3 before, /device:TPU:32 now
where the time goes in v3:
time: 56 us; the launch traced here: 55.8 us
  Pallas kernels  54.4 us (97%)
  local copies, waits for them, and re-layouts  1.38 us (2%)
    pallas_call x1, Pallas kernels, body(): pl.pallas_call(kernel, out_shape=jax.ShapeDtypeStruct((8, 16, 128), BF16)...  54.4 us
    unnamed x1, local copies, waits for them, and re-layouts  1.38 us

profile of v3, /device:TPU:32, one launch (start us, length us, event | category | flops | bytes accessed | tf_op | source)
XLA Modules:
  0.0 55.8 jit_solution(15821007177184880464)
XLA Ops:
  0.0 54.4 %triangles.1 = bf16[8,16,128]{2,1,0:T(8,128)(2,1)} custom-call(bf16[8,16,128]{2,1,0:T(8,128)(2,1)} %map_in.1, bf16[128,512]{1,0:T(8,128)(2,1)} %proj1_in.1, bf16[128,128]{1,0:T(8,128)(2,1)} %gate1_in.1, bf16[128,128]{1,0:T(8,128)(2,1)} %final1_in.1, bf16[128,512]{1,0:T(8,128)(2,1)} %proj2_in.1, bf16[128,128]{1,0:T(8,128)(2,1)} %gate2_in.1, ...), custom_call_target="tpu_custom_call" | custom-call | tf_op jit(solution)/shard_map/triangles/pallas_call | solution.py:319
  54.4 1.4 %copy.9 = bf16[8,16,128]{2,1,0:T(8,128)(2,1)} copy(bf16[8,16,128]{2,1,0:T(8,128)(2,1)} %triangles.1) | data formatting | bytes 65536

commit v4 on v3

v4 whole, which is shorter than its diff:
```python
import jax
import jax.numpy as jnp
from jax import lax
from jax.experimental import pallas as pl
from jax.experimental.pallas import tpu as pltpu
from jax.sharding import PartitionSpec as P

MESH = pl.DeviceIdType.MESH
F32 = jnp.float32
BF16 = jnp.bfloat16


def normalize(values):
    average = jnp.mean(values, axis=-1, keepdims=True)
    centred = values - average
    spread = jnp.mean(centred * centred, axis=-1, keepdims=True)
    return centred * lax.rsqrt(spread + 1e-05)


def prepare(block, proj_ref):
    normed = normalize(block.astype(F32)).astype(BF16)
    projected = jnp.dot(normed, proj_ref[...], preferred_element_type=F32)
    left = jax.nn.sigmoid(projected[:, 0:128]) * projected[:, 128:256]
    right = jax.nn.sigmoid(projected[:, 256:384]) * projected[:, 384:512]
    return left, right


def output_gate(block, gate_ref):
    normed = normalize(block.astype(F32)).astype(BF16)
    return jax.nn.sigmoid(jnp.dot(normed, gate_ref[...], preferred_element_type=F32))


def finish(block, summed, gate, final_ref):
    mixed = normalize(summed).astype(BF16)
    update = gate * jnp.dot(mixed, final_ref[...], preferred_element_type=F32)
    return (block.astype(F32) + update).astype(BF16)


def outer(a, b):
    a, b = a.astype(F32), b.astype(F32)
    i, j, k = 4, 8, a.shape[0] // 32
    a, b = a.reshape(i, k, 8, 128), b.reshape(j, k, 8, 128)
    total = None
    for n in range(k):
        term = a[:, None, n] * b[None, :, n]
        total = term if total is None else total + term
    return total


def kernel(
    map_in, proj1_in, gate1_in, final1_in, proj2_in, gate2_in, final2_in, out_ref,
    map_ref, proj1, gate1, final1, proj2, gate2, final2,
    send_l1, send_r1, left1, right1, send_p1, part1, own1, block1, middle,
    turned, send_l2, send_r2, left2, right2, send_p2, part2, block2,
    load, out_turn, out, in_turn, in_z, in_a_r1, in_b_r1, in_l1, in_p1, in_a_l2, in_b_l2, in_r2, in_p2, far,
):
    row, col = lax.axis_index("row"), lax.axis_index("col")
    y, zl, core = row // 8, row // 2 % 4, row % 2
    x, zh = col // 4, col % 4

    def at(x_, y_, zh_, zl_, core_):
        return (y_ * 8 + zl_ * 2 + core_, x_ * 4 + zh_)

    def plus(value, step):
        return (value + step) % 4

    def minus(value, step):
        return (value + 4 - step) % 4

    flat = x == y
    sibling = at(x, y, zh, zl, 1 - core)
    swapped = at(y, x, zh, zl, core)
    zl_sends, y_sends, x_sends, far_sends, near_sends = range(5)

    def copy(src, dst, send, recv, device):
        return pltpu.make_async_remote_copy(
            src_ref=src, dst_ref=dst, send_sem=send, recv_sem=recv, device_id=device, device_id_type=MESH
        )

    def push(src, dst, send, recv, device):
        copy(src, dst, send, recv, device).start()

    def push_unless(stays, src, dst, send, recv, device):
        @pl.when(jnp.logical_not(stays))
        def _():
            copy(src, dst, send, recv, device).start()

        @pl.when(stays)
        def _():
            pltpu.make_async_copy(src, dst, recv).start()

    def landed(like, recv):
        copy(like, like, out_turn.at[0], recv, sibling).wait_recv()

    def sent(like, send):
        copy(like, like, send, in_turn.at[0], sibling).wait_send()

    first_loads = [
        pltpu.make_async_copy(map_in, map_ref, load.at[0]),
        pltpu.make_async_copy(proj1_in, proj1, load.at[1]),
    ]
    later_loads = [
        pltpu.make_async_copy(src, dst, load.at[2])
        for src, dst in (
            (gate1_in, gate1), (final1_in, final1), (proj2_in, proj2), (gate2_in, gate2), (final2_in, final2),
        )
    ]

    barrier = pltpu.get_barrier_semaphore()
    greeted = []

    def greet(device, stays=None):
        def signal():
            pl.semaphore_signal(barrier, inc=1, device_id=device, device_id_type=MESH)

        if stays is None:
            signal()
            greeted.append(1)
        else:
            pl.when(jnp.logical_not(stays))(signal)
            greeted.append(1 - stays.astype(jnp.int32))

    for step in (2, 1, 3):
        for side in (0, 1):
            other = (core + side) % 2
            if step != 2:
                greet(at(x, y, plus(zh, step), zl, other))
            greet(at(x, plus(y, step), zh, zl, other))
        greet(at(plus(x, step), y, zh, zl, core))
        greet(at(x, y, zh, plus(zl, step), core))
    greet(sibling)
    greet(swapped, flat)

    for c in first_loads + later_loads:
        c.start()

    for c in first_loads:
        c.wait()
    left, right = prepare(map_ref[...].reshape(128, 128), proj1)
    send_r1[...] = right.astype(BF16)
    right1[x, zl] = send_r1[...]
    send_l1[...] = left.astype(BF16)

    pl.semaphore_wait(barrier, sum(greeted))

    for step in (1, 3):
        pl.semaphore_signal(far, inc=1, device_id=at(x, y, plus(zh, step), zl, core), device_id_type=MESH)
    push_unless(flat, send_l1, left1.at[2 * x + core], out_turn.at[0], in_turn.at[0], swapped)
    for step in (2, 1, 3):
        push(send_r1, right1.at[x, zl], out.at[0, zl_sends], in_a_r1.at[zl], at(x, y, zh, plus(zl, step), core))

    def right_over_x(from_zl):
        piece = right1.at[x, from_zl]
        for hop in (2, 1, 3):
            push(piece, piece, out.at[0, x_sends], in_b_r1.at[from_zl], at(plus(x, hop), y, zh, zl, core))

    piece = left1.at[2 * y + core]
    landed(piece, in_turn.at[0])
    for step in (2, 1, 3, 0):
        for side in (1, 0):
            if step or side:
                push(piece, piece, out.at[0, y_sends], in_l1, at(x, plus(y, step), zh, zl, (core + side) % 2))
    right_over_x(zl)
    for step in (2, 1, 3, 0):
        from_zl = plus(zh, step)

        @pl.when(from_zl != zl)
        def _(from_zl=from_zl):
            landed(right1.at[x, from_zl], in_a_r1.at[from_zl])
            right_over_x(from_zl)

    push_unless(flat, map_ref, block1, out_turn.at[1], in_z.at[0], swapped)

    landed(left1.at[0:7], in_l1)
    for step in (2, 1, 3, 0):
        to_zh = plus(zh, step)
        landed(right1.at[0, 0:3], in_b_r1.at[to_zh])

        def four_rows(n, _, step=step, to_zh=to_zh):
            half, quarter = n // 2, n % 2
            total = None
            for from_x in range(4):
                term = outer(
                    left1[2 * from_x + half, pl.ds(pl.multiple_of(quarter * 64, 64), 64), :], right1[from_x, to_zh]
                )
                total = term if total is None else total + term
            part = jnp.sum(total, axis=2).reshape(32, 128)
            rows = pl.ds(pl.multiple_of(quarter * 32, 32), 32)
            send_p1[2 * step + half, rows, :] = part.astype(BF16)
            if step == 0:
                own1[half, rows, :] = part
            return 0

        lax.fori_loop(0, 4, four_rows, 0)
        if step == 2:
            pl.semaphore_wait(far, 2)
        for side in (0, 1):
            to = (core + side) % 2
            if step or side:
                push(send_p1.at[2 * step + to], part1.at[2 * step + core], out.at[0, far_sends], in_p1,
                     at(x, y, to_zh, zl, to))

    landed(block1, in_z.at[0])
    pltpu.make_async_copy(left2.at[0:2], left2.at[0:2], load.at[2]).wait()
    block = block1[...].reshape(128, 128)
    gate = output_gate(block, gate1)
    landed(part1.at[0:7], in_p1)
    halves = []
    for side in range(2):
        near = jnp.where(core == side, own1[side], part1[0 + side].astype(F32))
        rest = part1[2 + side].astype(F32) + part1[4 + side].astype(F32) + part1[6 + side].astype(F32)
        halves.append((near + rest).reshape(8, 1, 8, 128))
    summed = jnp.concatenate(halves, axis=1).reshape(128, 128)
    block = finish(block, summed, gate, final1)
    middle[...] = block.reshape(8, 16, 128)

    left, right = prepare(block, proj2)
    turned[0] = left
    turned[1] = right
    for which, send_ref in ((0, send_l2), (1, send_r2)):
        for j in range(0, 16, 2):
            pair = [turned[which, pl.ds(j + k, 8, stride=16), :] for k in range(2)]
            send_ref[j // 8, (j % 8) * 8 : (j % 8) * 8 + 16, :] = jnp.concatenate(pair, axis=0).astype(BF16)
    push_unless(flat, send_r2, right2.at[2 * x + core], out_turn.at[2], in_turn.at[1], swapped)
    left2[x, zh, core] = send_l2[core]
    for step in (0, 1, 3, 2):
        for side in (0, 1):
            to = (core + side) % 2
            if step or side:
                push(send_l2.at[to], left2.at[x, zh, core], out.at[1, far_sends], in_a_l2.at[zh],
                     at(x, y, plus(zh, step), zl, to))
    push_unless(flat, middle, block2, out_turn.at[3], in_z.at[1], swapped)

    def left_over_x(step):
        from_zh = minus(zh, step)
        piece = left2.at[x, from_zh]
        landed(piece if step else left2.at[x, from_zh, 1 - core], in_a_l2.at[from_zh])
        for hop in (2, 1, 3):
            push(piece, piece, out.at[1, x_sends], in_b_l2.at[from_zh], at(plus(x, hop), y, zh, zl, core))

    left_over_x(0)
    piece = right2.at[2 * y + core]
    landed(piece, in_turn.at[1])
    for step in (2, 1, 3, 0):
        for side in (1, 0):
            if step or side:
                push(piece, piece, out.at[1, y_sends], in_r2, at(x, plus(y, step), zh, zl, (core + side) % 2))
    left_over_x(1)
    left_over_x(3)
    left_over_x(2)
    landed(right2.at[0:7], in_r2)

    for step in (0, 1, 3, 2):
        from_zh = minus(zh, step)
        landed(left2.at[0, 0:3], in_b_l2.at[from_zh])

        def four_rows2(quarter, _, step=step, from_zh=from_zh):
            parts = []
            for j_half in range(2):
                total = None
                for from_x in range(4):
                    for other in range(2):
                        term = outer(
                            left2[from_x, from_zh, other, pl.ds(pl.multiple_of(quarter * 32, 32), 32), :],
                            right2[2 * from_x + other, j_half],
                        )
                        total = term if total is None else total + term
                parts.append(jnp.sum(total, axis=2).reshape(4, 1, 8, 128))
            send_p2[step, quarter] = jnp.concatenate(parts, axis=1).reshape(64, 128).astype(BF16)
            return 0

        lax.fori_loop(0, 2, four_rows2, 0)
        push_unless(from_zh == zl, send_p2.at[step], part2.at[zl], out.at[1, near_sends], in_p2,
                    at(x, y, zh, from_zh, core))

    landed(block2, in_z.at[1])
    block = block2[...].reshape(128, 128)
    gate = output_gate(block, gate2)
    landed(part2, in_p2)
    summed = [part2[n].astype(F32).reshape(128, 128) for n in range(4)]
    summed = (summed[0] + summed[1]) + (summed[2] + summed[3])
    out_ref[...] = finish(block, summed, gate, final2).reshape(8, 16, 128)

    sent(right1.at[0, 0:3], out.at[0, zl_sends])
    sent(left1.at[0:7], out.at[0, y_sends])
    sent(right1.at[0:3], out.at[0, x_sends])
    sent(send_p1.at[0:7], out.at[0, far_sends])
    sent(right2.at[0:7], out.at[1, y_sends])
    sent(left2.at[0:3], out.at[1, x_sends])
    sent(part1.at[0:7], out.at[1, far_sends])
    sent(send_p2.at[0:3], out.at[1, near_sends])

    @pl.when(jnp.logical_not(flat))
    def _():
        sent(send_l1, out_turn.at[0])
        sent(block1, out_turn.at[1])
        sent(send_r2, out_turn.at[2])
        sent(block2, out_turn.at[3])


def body(*args):
    dma = pltpu.SemaphoreType.DMA
    weights = [pltpu.VMEM((128, 512), BF16), pltpu.VMEM((128, 128), BF16), pltpu.VMEM((128, 128), BF16)]
    tile = pltpu.VMEM((8, 16, 128), BF16)
    return pl.pallas_call(
        kernel,
        out_shape=jax.ShapeDtypeStruct((8, 16, 128), BF16),
        in_specs=[pl.BlockSpec(memory_space=pl.ANY)] * 7,
        out_specs=pl.BlockSpec(memory_space=pltpu.VMEM),
        scratch_shapes=[tile, *weights, *weights]
        + [pltpu.VMEM((128, 128), BF16)] * 2
        + [pltpu.VMEM((8, 128, 128), BF16), pltpu.VMEM((4, 4, 128, 128), BF16)]
        + [pltpu.VMEM((8, 64, 128), BF16)] * 2
        + [pltpu.VMEM((2, 64, 128), F32), tile, tile]
        + [pltpu.VMEM((2, 128, 128), F32)]
        + [pltpu.VMEM((2, 64, 128), BF16)] * 2
        + [pltpu.VMEM((4, 4, 2, 64, 128), BF16), pltpu.VMEM((8, 2, 64, 128), BF16)]
        + [pltpu.VMEM((4, 2, 64, 128), BF16)] * 2
        + [tile]
        + [dma((3,)), dma((4,)), dma((2, 5)), dma((2,)), dma((2,)), dma((4,)), dma((4,)), dma, dma]
        + [dma((4,)), dma((4,)), dma, dma, pltpu.SemaphoreType.REGULAR],
        compiler_params=pltpu.CompilerParams(
            collective_id=0, has_side_effects=True, vmem_limit_bytes=32 * 1024 * 1024
        ),
        name="triangles",
    )(*[pltpu.with_memory_space_constraint(a, pltpu.HBM) for a in args])


def solution(mesh):
    return jax.shard_map(
        body,
        mesh=mesh,
        in_specs=(P("row", "col", None), P(), P(), P(), P(), P(), P()),
        out_specs=P("row", "col", None),
        check_vma=False,
    )
```

time: 56 us -> 52.1 us (0.930)
  the two profiles are of different devices: /device:TPU:32 before, /device:TPU:1 now
where the time goes in v4:
time: 52.1 us; the launch traced here: 51.2 us
  Pallas kernels  50.6 us (97%)
  local copies, waits for them, and re-layouts  0.62 us (1%)
    pallas_call x1, Pallas kernels, body(): pl.pallas_call(kernel, out_shape=jax.ShapeDtypeStruct((8, 16, 128), BF16)...  50.6 us

profile of v4, /device:TPU:1, one launch (start us, length us, event | category | flops | bytes accessed | tf_op | source)
XLA Modules:
  0.0 51.2 jit_solution(9199392306386170094)
XLA Ops:
  0.0 50.6 %triangles.1 = bf16[8,16,128]{2,1,0:T(8,128)(2,1)S(1)} custom-call(bf16[8,16,128]{2,1,0:T(8,128)(2,1)} %map_in.1, bf16[128,512]{1,0:T(8,128)(2,1)} %proj1_in.1, bf16[128,128]{1,0:T(8,128)(2,1)} %gate1_in.1, bf16[128,128]{1,0:T(8,128)(2,1)} %final1_in.1, bf16[128,512]{1,0:T(8,128)(2,1)} %proj2_in.1, bf16[128,128]{1,0:T(8,128)(2,1)} %gate2_in.1, ...), custom_call_target="tpu_custom_call" | custom-call | tf_op jit(solution)/shard_map/triangles/pallas_call | solution.py:305
  50.6 0.6 %copy.9 = bf16[8,16,128]{2,1,0:T(8,128)(2,1)} copy(bf16[8,16,128]{2,1,0:T(8,128)(2,1)S(1)} %triangles.1) | data formatting | bytes 65536

commit v5 on v4

--- a/solution.py
+++ b/solution.py
@@ -155,50 +155,58 @@
             push(piece, piece, out.at[0, x_sends], in_b_r1.at[from_zl], at(plus(x, hop), y, zh, zl, core))
 
     piece = left1.at[2 * y + core]
-    landed(piece, in_turn.at[0])
-    for step in (2, 1, 3, 0):
-        for side in (1, 0):
+
+    def left_over_y(side):
+        for step in (2, 1, 3, 0):
             if step or side:
-                push(piece, piece, out.at[0, y_sends], in_l1, at(x, plus(y, step), zh, zl, (core + side) % 2))
-    right_over_x(zl)
-    for step in (2, 1, 3, 0):
+                push(piece, piece, out.at[0, y_sends], in_l1.at[side], at(x, plus(y, step), zh, zl, (core + side) % 2))
+
+    def right_from(step):
         from_zl = plus(zh, step)
 
         @pl.when(from_zl != zl)
-        def _(from_zl=from_zl):
+        def _():
             landed(right1.at[x, from_zl], in_a_r1.at[from_zl])
             right_over_x(from_zl)
 
+    right_over_x(zl)
+    landed(piece, in_turn.at[0])
+    left_over_y(0)
+    left_over_y(1)
+    right_from(2)
+    right_from(1)
+    right_from(3)
+    right_from(0)
     push_unless(flat, map_ref, block1, out_turn.at[1], in_z.at[0], swapped)
 
-    landed(left1.at[0:7], in_l1)
-    for step in (2, 1, 3, 0):
-        to_zh = plus(zh, step)
-        landed(right1.at[0, 0:3], in_b_r1.at[to_zh])
-
-        def four_rows(n, _, step=step, to_zh=to_zh):
-            half, quarter = n // 2, n % 2
-            total = None
-            for from_x in range(4):
-                term = outer(
-                    left1[2 * from_x + half, pl.ds(pl.multiple_of(quarter * 64, 64), 64), :], right1[from_x, to_zh]
-                )
-                total = term if total is None else total + term
-            part = jnp.sum(total, axis=2).reshape(32, 128)
-            rows = pl.ds(pl.multiple_of(quarter * 32, 32), 32)
-            send_p1[2 * step + half, rows, :] = part.astype(BF16)
-            if step == 0:
-                own1[half, rows, :] = part
-            return 0
-
-        lax.fori_loop(0, 4, four_rows, 0)
-        if step == 2:
-            pl.semaphore_wait(far, 2)
-        for side in (0, 1):
-            to = (core + side) % 2
+    for side in (0, 1):
+        half = (core + side) % 2
+        landed(left1.at[0 : 3 + side], in_l1.at[side])
+        for step in (2, 1, 3, 0):
+            to_zh = plus(zh, step)
+            if side == 0:
+                landed(right1.at[0, 0:3], in_b_r1.at[to_zh])
+
+            def four_rows(quarter, _, step=step, to_zh=to_zh, half=half):
+                total = None
+                for from_x in range(4):
+                    term = outer(
+                        left1[2 * from_x + half, pl.ds(pl.multiple_of(quarter * 64, 64), 64), :], right1[from_x, to_zh]
+                    )
+                    total = term if total is None else total + term
+                part = jnp.sum(total, axis=2).reshape(32, 128)
+                rows = pl.ds(pl.multiple_of(quarter * 32, 32), 32)
+                send_p1[2 * step + half, rows, :] = part.astype(BF16)
+                if step == 0:
+                    own1[half, rows, :] = part
+                return 0
+
+            lax.fori_loop(0, 2, four_rows, 0)
+            if step == 2 and side == 0:
+                pl.semaphore_wait(far, 2)
             if step or side:
-                push(send_p1.at[2 * step + to], part1.at[2 * step + core], out.at[0, far_sends], in_p1,
-                     at(x, y, to_zh, zl, to))
+                push(send_p1.at[2 * step + half], part1.at[2 * step + core], out.at[0, far_sends], in_p1,
+                     at(x, y, to_zh, zl, half))
 
     landed(block1, in_z.at[0])
     pltpu.make_async_copy(left2.at[0:2], left2.at[0:2], load.at[2]).wait()
@@ -317,7 +325,7 @@
         + [pltpu.VMEM((4, 4, 2, 64, 128), BF16), pltpu.VMEM((8, 2, 64, 128), BF16)]
         + [pltpu.VMEM((4, 2, 64, 128), BF16)] * 2
         + [tile]
-        + [dma((3,)), dma((4,)), dma((2, 5)), dma((2,)), dma((2,)), dma((4,)), dma((4,)), dma, dma]
+        + [dma((3,)), dma((4,)), dma((2, 5)), dma((2,)), dma((2,)), dma((4,)), dma((4,)), dma((2,)), dma]
         + [dma((4,)), dma((4,)), dma, dma, pltpu.SemaphoreType.REGULAR],
         compiler_params=pltpu.CompilerParams(
             collective_id=0, has_side_effects=True, vmem_limit_bytes=32 * 1024 * 1024

time: 52.1 us -> 50.3 us (0.965)
  Pallas kernels: 50.6 us -> 49.1 us
    pallas_call x1, Pallas kernels: 50.6 us -> 49.1 us  [body(): pl.pallas_call(kernel, out_shape=jax.ShapeDtypeStruct((8, 16, 128), BF16)...]
where the time goes in v5:
time: 50.3 us; the launch traced here: 49.7 us
  Pallas kernels  49.1 us (98%)
  local copies, waits for them, and re-layouts  0.62 us (1%)
    pallas_call x1, Pallas kernels, body(): pl.pallas_call(kernel, out_shape=jax.ShapeDtypeStruct((8, 16, 128), BF16)...  49.1 us

profile of v5, /device:TPU:1, one launch (start us, length us, event | category | flops | bytes accessed | tf_op | source)
XLA Modules:
  0.0 49.7 jit_solution(4796351829929464731)
XLA Ops:
  0.0 49.1 %triangles.1 = bf16[8,16,128]{2,1,0:T(8,128)(2,1)S(1)} custom-call(bf16[8,16,128]{2,1,0:T(8,128)(2,1)} %map_in.1, bf16[128,512]{1,0:T(8,128)(2,1)} %proj1_in.1, bf16[128,128]{1,0:T(8,128)(2,1)} %gate1_in.1, bf16[128,128]{1,0:T(8,128)(2,1)} %final1_in.1, bf16[128,512]{1,0:T(8,128)(2,1)} %proj2_in.1, bf16[128,128]{1,0:T(8,128)(2,1)} %gate2_in.1, ...), custom_call_target="tpu_custom_call" | custom-call | tf_op jit(solution)/shard_map/triangles/pallas_call | solution.py:313
  49.1 0.6 %copy.9 = bf16[8,16,128]{2,1,0:T(8,128)(2,1)} copy(bf16[8,16,128]{2,1,0:T(8,128)(2,1)S(1)} %triangles.1) | data formatting | bytes 65536

commit v6 on v5

--- a/solution.py
+++ b/solution.py
@@ -50,7 +50,7 @@
 def kernel(
     map_in, proj1_in, gate1_in, final1_in, proj2_in, gate2_in, final2_in, out_ref,
     map_ref, proj1, gate1, final1, proj2, gate2, final2,
-    send_l1, send_r1, left1, right1, send_p1, part1, own1, block1, middle,
+    send_z, send_l1, send_r1, left1, right1, send_p1, part1, own1, block1, middle,
     turned, send_l2, send_r2, left2, right2, send_p2, part2, block2,
     load, out_turn, out, in_turn, in_z, in_a_r1, in_b_r1, in_l1, in_p1, in_a_l2, in_b_l2, in_r2, in_p2, far,
 ):
@@ -121,15 +121,15 @@
             greeted.append(1 - stays.astype(jnp.int32))
 
     for step in (2, 1, 3):
+        if step != 2:
+            greet(at(x, y, plus(zh, step), zl, core))
         for side in (0, 1):
-            other = (core + side) % 2
-            if step != 2:
-                greet(at(x, y, plus(zh, step), zl, other))
-            greet(at(x, plus(y, step), zh, zl, other))
+            greet(at(x, plus(y, step), zh, zl, (core + side) % 2))
         greet(at(plus(x, step), y, zh, zl, core))
         greet(at(x, y, zh, plus(zl, step), core))
     greet(sibling)
     greet(swapped, flat)
+    greet(at(y, x, zh, zl, 1 - core))
 
     for c in first_loads + later_loads:
         c.start()
@@ -137,6 +137,9 @@
     for c in first_loads:
         c.wait()
     left, right = prepare(map_ref[...].reshape(128, 128), proj1)
+    columns = map_ref[...].astype(F32).reshape(8, 2, 8, 128)
+    for side in range(2):
+        send_z[side] = columns[:, side].reshape(64, 128).astype(BF16)
     send_r1[...] = right.astype(BF16)
     right1[x, zl] = send_r1[...]
     send_l1[...] = left.astype(BF16)
@@ -177,7 +180,8 @@
     right_from(1)
     right_from(3)
     right_from(0)
-    push_unless(flat, map_ref, block1, out_turn.at[1], in_z.at[0], swapped)
+    push_unless(flat, send_z.at[core], block1.at[core], out_turn.at[1], in_z.at[0], swapped)
+    push(send_z.at[1 - core], block1.at[core], out.at[0, near_sends], in_z.at[0], at(y, x, zh, zl, 1 - core))
 
     for side in (0, 1):
         half = (core + side) % 2
@@ -204,45 +208,42 @@
             lax.fori_loop(0, 2, four_rows, 0)
             if step == 2 and side == 0:
                 pl.semaphore_wait(far, 2)
-            if step or side:
-                push(send_p1.at[2 * step + half], part1.at[2 * step + core], out.at[0, far_sends], in_p1,
-                     at(x, y, to_zh, zl, half))
+            if step:
+                push(send_p1.at[2 * step + half], part1.at[2 * step + half], out.at[0, far_sends], in_p1,
+                     at(x, y, to_zh, zl, core))
 
     landed(block1, in_z.at[0])
     pltpu.make_async_copy(left2.at[0:2], left2.at[0:2], load.at[2]).wait()
     block = block1[...].reshape(128, 128)
     gate = output_gate(block, gate1)
-    landed(part1.at[0:7], in_p1)
-    halves = []
-    for side in range(2):
-        near = jnp.where(core == side, own1[side], part1[0 + side].astype(F32))
-        rest = part1[2 + side].astype(F32) + part1[4 + side].astype(F32) + part1[6 + side].astype(F32)
-        halves.append((near + rest).reshape(8, 1, 8, 128))
-    summed = jnp.concatenate(halves, axis=1).reshape(128, 128)
+    landed(part1.at[0:6], in_p1)
+    halves = [
+        (own1[n] + part1[2 + n].astype(F32)) + (part1[4 + n].astype(F32) + part1[6 + n].astype(F32)) for n in range(2)
+    ]
+    summed = jnp.concatenate(halves, axis=0)
     block = finish(block, summed, gate, final1)
-    middle[...] = block.reshape(8, 16, 128)
+    middle[...] = block.reshape(2, 64, 128)
 
     left, right = prepare(block, proj2)
     turned[0] = left
     turned[1] = right
     for which, send_ref in ((0, send_l2), (1, send_r2)):
-        for j in range(0, 16, 2):
-            pair = [turned[which, pl.ds(j + k, 8, stride=16), :] for k in range(2)]
-            send_ref[j // 8, (j % 8) * 8 : (j % 8) * 8 + 16, :] = jnp.concatenate(pair, axis=0).astype(BF16)
+        for half in range(2):
+            for j in range(0, 8, 2):
+                pair = [turned[which, pl.ds(64 * half + j + k, 8, stride=8), :] for k in range(2)]
+                send_ref[half, j * 8 : j * 8 + 16, :] = jnp.concatenate(pair, axis=0).astype(BF16)
     push_unless(flat, send_r2, right2.at[2 * x + core], out_turn.at[2], in_turn.at[1], swapped)
-    left2[x, zh, core] = send_l2[core]
-    for step in (0, 1, 3, 2):
-        for side in (0, 1):
-            to = (core + side) % 2
-            if step or side:
-                push(send_l2.at[to], left2.at[x, zh, core], out.at[1, far_sends], in_a_l2.at[zh],
-                     at(x, y, plus(zh, step), zl, to))
-    push_unless(flat, middle, block2, out_turn.at[3], in_z.at[1], swapped)
+    left2[x, zh] = send_l2[...]
+    for step in (1, 3, 2):
+        push(send_l2, left2.at[x, zh], out.at[1, far_sends], in_a_l2.at[zh], at(x, y, plus(zh, step), zl, core))
+    push_unless(flat, middle.at[core], block2.at[core], out_turn.at[3], in_z.at[1], swapped)
+    push(middle.at[1 - core], block2.at[core], out.at[1, zl_sends], in_z.at[1], at(y, x, zh, zl, 1 - core))
 
     def left_over_x(step):
         from_zh = minus(zh, step)
         piece = left2.at[x, from_zh]
-        landed(piece if step else left2.at[x, from_zh, 1 - core], in_a_l2.at[from_zh])
+        if step:
+            landed(piece, in_a_l2.at[from_zh])
         for hop in (2, 1, 3):
             push(piece, piece, out.at[1, x_sends], in_b_l2.at[from_zh], at(plus(x, hop), y, zh, zl, core))
 
@@ -270,19 +271,20 @@
                     for other in range(2):
                         term = outer(
                             left2[from_x, from_zh, other, pl.ds(pl.multiple_of(quarter * 32, 32), 32), :],
-                            right2[2 * from_x + other, j_half],
+                            right2[2 * from_x + j_half, other],
                         )
                         total = term if total is None else total + term
                 parts.append(jnp.sum(total, axis=2).reshape(4, 1, 8, 128))
             send_p2[step, quarter] = jnp.concatenate(parts, axis=1).reshape(64, 128).astype(BF16)
             return 0
 
-        lax.fori_loop(0, 2, four_rows2, 0)
-        push_unless(from_zh == zl, send_p2.at[step], part2.at[zl], out.at[1, near_sends], in_p2,
-                    at(x, y, zh, from_zh, core))
+        for quarter in range(2):
+            four_rows2(quarter, 0)
+            push_unless(from_zh == zl, send_p2.at[step, quarter], part2.at[zl, quarter], out.at[1, near_sends], in_p2,
+                        at(x, y, zh, from_zh, core))
 
     landed(block2, in_z.at[1])
-    block = block2[...].reshape(128, 128)
+    block = jnp.concatenate([block2[n].astype(F32).reshape(8, 1, 8, 128) for n in range(2)], axis=1).reshape(128, 128)
     gate = output_gate(block, gate2)
     landed(part2, in_p2)
     summed = [part2[n].astype(F32).reshape(128, 128) for n in range(4)]
@@ -292,18 +294,20 @@
     sent(right1.at[0, 0:3], out.at[0, zl_sends])
     sent(left1.at[0:7], out.at[0, y_sends])
     sent(right1.at[0:3], out.at[0, x_sends])
-    sent(send_p1.at[0:7], out.at[0, far_sends])
+    sent(send_p1.at[0:6], out.at[0, far_sends])
+    sent(send_z.at[0], out.at[0, near_sends])
     sent(right2.at[0:7], out.at[1, y_sends])
     sent(left2.at[0:3], out.at[1, x_sends])
-    sent(part1.at[0:7], out.at[1, far_sends])
+    sent(left2.at[0, 0:3], out.at[1, far_sends])
+    sent(middle.at[0], out.at[1, zl_sends])
     sent(send_p2.at[0:3], out.at[1, near_sends])
 
     @pl.when(jnp.logical_not(flat))
     def _():
         sent(send_l1, out_turn.at[0])
-        sent(block1, out_turn.at[1])
+        sent(block1.at[0], out_turn.at[1])
         sent(send_r2, out_turn.at[2])
-        sent(block2, out_turn.at[3])
+        sent(block2.at[0], out_turn.at[3])
 
 
 def body(*args):
@@ -316,15 +320,16 @@
         in_specs=[pl.BlockSpec(memory_space=pl.ANY)] * 7,
         out_specs=pl.BlockSpec(memory_space=pltpu.VMEM),
         scratch_shapes=[tile, *weights, *weights]
+        + [pltpu.VMEM((2, 64, 128), BF16)]
         + [pltpu.VMEM((128, 128), BF16)] * 2
         + [pltpu.VMEM((8, 128, 128), BF16), pltpu.VMEM((4, 4, 128, 128), BF16)]
         + [pltpu.VMEM((8, 64, 128), BF16)] * 2
-        + [pltpu.VMEM((2, 64, 128), F32), tile, tile]
+        + [pltpu.VMEM((2, 64, 128), F32)] + [pltpu.VMEM((2, 64, 128), BF16)] * 2
         + [pltpu.VMEM((2, 128, 128), F32)]
         + [pltpu.VMEM((2, 64, 128), BF16)] * 2
         + [pltpu.VMEM((4, 4, 2, 64, 128), BF16), pltpu.VMEM((8, 2, 64, 128), BF16)]
         + [pltpu.VMEM((4, 2, 64, 128), BF16)] * 2
-        + [tile]
+        + [pltpu.VMEM((2, 64, 128), BF16)]
         + [dma((3,)), dma((4,)), dma((2, 5)), dma((2,)), dma((2,)), dma((4,)), dma((4,)), dma((2,)), dma]
         + [dma((4,)), dma((4,)), dma, dma, pltpu.SemaphoreType.REGULAR],
         compiler_params=pltpu.CompilerParams(

time: 50.3 us -> 48.7 us (0.968)
  Pallas kernels: 49.1 us -> 47.9 us
    pallas_call x1, Pallas kernels: 49.1 us -> 47.9 us  [body(): pl.pallas_call(kernel, out_shape=jax.ShapeDtypeStruct((8, 16, 128), BF16)...]
where the time goes in v6:
time: 48.7 us; the launch traced here: 48.6 us
  Pallas kernels  47.9 us (98%)
  local copies, waits for them, and re-layouts  0.62 us (1%)
    pallas_call x1, Pallas kernels, body(): pl.pallas_call(kernel, out_shape=jax.ShapeDtypeStruct((8, 16, 128), BF16)...  47.9 us

profile of v6, /device:TPU:1, one launch (start us, length us, event | category | flops | bytes accessed | tf_op | source)
XLA Modules:
  0.0 48.6 jit_solution(7986021764205781659)
XLA Ops:
  0.0 47.9 %triangles.1 = bf16[8,16,128]{2,1,0:T(8,128)(2,1)S(1)} custom-call(bf16[8,16,128]{2,1,0:T(8,128)(2,1)} %map_in.1, bf16[128,512]{1,0:T(8,128)(2,1)} %proj1_in.1, bf16[128,128]{1,0:T(8,128)(2,1)} %gate1_in.1, bf16[128,128]{1,0:T(8,128)(2,1)} %final1_in.1, bf16[128,512]{1,0:T(8,128)(2,1)} %proj2_in.1, bf16[128,128]{1,0:T(8,128)(2,1)} %gate2_in.1, ...), custom_call_target="tpu_custom_call" | custom-call | tf_op jit(solution)/shard_map/triangles/pallas_call | solution.py:317
  47.9 0.6 %copy.9 = bf16[8,16,128]{2,1,0:T(8,128)(2,1)} copy(bf16[8,16,128]{2,1,0:T(8,128)(2,1)S(1)} %triangles.1) | data formatting | bytes 65536

commit v7 on v6

--- a/solution.py
+++ b/solution.py
@@ -154,13 +154,13 @@
 
     def right_over_x(from_zl):
         piece = right1.at[x, from_zl]
-        for hop in (2, 1, 3):
+        for hop in (1, 3, 2):
             push(piece, piece, out.at[0, x_sends], in_b_r1.at[from_zl], at(plus(x, hop), y, zh, zl, core))
 
     piece = left1.at[2 * y + core]
 
     def left_over_y(side):
-        for step in (2, 1, 3, 0):
+        for step in (1, 3, 2, 0):
             if step or side:
                 push(piece, piece, out.at[0, y_sends], in_l1.at[side], at(x, plus(y, step), zh, zl, (core + side) % 2))
 
@@ -244,7 +244,7 @@
         piece = left2.at[x, from_zh]
         if step:
             landed(piece, in_a_l2.at[from_zh])
-        for hop in (2, 1, 3):
+        for hop in (1, 3, 2):
             push(piece, piece, out.at[1, x_sends], in_b_l2.at[from_zh], at(plus(x, hop), y, zh, zl, core))
 
     left_over_x(0)

time: 48.7 us -> 48.8 us (level)
  no operation moved by 1% of the time
where the time goes in v7:
time: 48.8 us; the launch traced here: 48.6 us
  Pallas kernels  48 us (98%)
  local copies, waits for them, and re-layouts  0.62 us (1%)
    pallas_call x1, Pallas kernels, body(): pl.pallas_call(kernel, out_shape=jax.ShapeDtypeStruct((8, 16, 128), BF16)...  48 us

profile of v7, /device:TPU:1, one launch (start us, length us, event | category | flops | bytes accessed | tf_op | source)
XLA Modules:
  0.0 48.6 jit_solution(10144864946760838732)
XLA Ops:
  0.0 48.0 %triangles.1 = bf16[8,16,128]{2,1,0:T(8,128)(2,1)S(1)} custom-call(bf16[8,16,128]{2,1,0:T(8,128)(2,1)} %map_in.1, bf16[128,512]{1,0:T(8,128)(2,1)} %proj1_in.1, bf16[128,128]{1,0:T(8,128)(2,1)} %gate1_in.1, bf16[128,128]{1,0:T(8,128)(2,1)} %final1_in.1, bf16[128,512]{1,0:T(8,128)(2,1)} %proj2_in.1, bf16[128,128]{1,0:T(8,128)(2,1)} %gate2_in.1, ...), custom_call_target="tpu_custom_call" | custom-call | tf_op jit(solution)/shard_map/triangles/pallas_call | solution.py:317
  48.0 0.6 %copy.9 = bf16[8,16,128]{2,1,0:T(8,128)(2,1)} copy(bf16[8,16,128]{2,1,0:T(8,128)(2,1)S(1)} %triangles.1) | data formatting | bytes 65536

commit v8 on v7

--- a/solution.py
+++ b/solution.py
@@ -234,7 +234,7 @@
                 send_ref[half, j * 8 : j * 8 + 16, :] = jnp.concatenate(pair, axis=0).astype(BF16)
     push_unless(flat, send_r2, right2.at[2 * x + core], out_turn.at[2], in_turn.at[1], swapped)
     left2[x, zh] = send_l2[...]
-    for step in (1, 3, 2):
+    for step in (2, 1, 3):
         push(send_l2, left2.at[x, zh], out.at[1, far_sends], in_a_l2.at[zh], at(x, y, plus(zh, step), zl, core))
     push_unless(flat, middle.at[core], block2.at[core], out_turn.at[3], in_z.at[1], swapped)
     push(middle.at[1 - core], block2.at[core], out.at[1, zl_sends], in_z.at[1], at(y, x, zh, zl, 1 - core))

time: 48.8 us -> 48.9 us (level)
  no operation moved by 1% of the time
where the time goes in v8:
time: 48.9 us; the launch traced here: 48.6 us
  Pallas kernels  48 us (98%)
  local copies, waits for them, and re-layouts  0.62 us (1%)
    pallas_call x1, Pallas kernels, body(): pl.pallas_call(kernel, out_shape=jax.ShapeDtypeStruct((8, 16, 128), BF16)...  48 us

profile of v8, /device:TPU:1, one launch (start us, length us, event | category | flops | bytes accessed | tf_op | source)
XLA Modules:
  0.0 48.6 jit_solution(9178936376279919495)
XLA Ops:
  0.0 48.0 %triangles.1 = bf16[8,16,128]{2,1,0:T(8,128)(2,1)S(1)} custom-call(bf16[8,16,128]{2,1,0:T(8,128)(2,1)} %map_in.1, bf16[128,512]{1,0:T(8,128)(2,1)} %proj1_in.1, bf16[128,128]{1,0:T(8,128)(2,1)} %gate1_in.1, bf16[128,128]{1,0:T(8,128)(2,1)} %final1_in.1, bf16[128,512]{1,0:T(8,128)(2,1)} %proj2_in.1, bf16[128,128]{1,0:T(8,128)(2,1)} %gate2_in.1, ...), custom_call_target="tpu_custom_call" | custom-call | tf_op jit(solution)/shard_map/triangles/pallas_call | solution.py:317
  48.0 0.6 %copy.9 = bf16[8,16,128]{2,1,0:T(8,128)(2,1)} copy(bf16[8,16,128]{2,1,0:T(8,128)(2,1)S(1)} %triangles.1) | data formatting | bytes 65536
